TPU v7x, 128 devices: a whole 4x4x4 slice. The times are simulated.
128 devices in a mesh: slide: 16 (over z_hi, x, core), ctx: 8 (over y, z_lo).
Axes of the slice: x: 4, y: 4, z: 4 (z_hi: 2, z_lo: 2; z = z_hi * 2 + z_lo), core: 2. Of those that a mesh axis runs over, the one named last changes fastest.
Arguments:
- tile_rows: bfloat16 [65536, 768], P(('slide', 'ctx')), may hold values from -6 to 6
- tile_slot: int32 [128, 512], P(('slide', 'ctx')), may hold values from 0 to 65535, as said below
- lengths: int32 [16], P('slide'), may hold values from 1365 to 4096, as said below
- ln_gain_attn: float32 [768], replicated, may hold values from 0.5 to 1.5
- w_query: bfloat16 [768, 768], P('slide'), may hold values from -1 to 1
- w_kv: bfloat16 [768, 1536], P('slide'), may hold values from -2 to 2
- w_out: bfloat16 [768, 768], P('slide'), may hold values from -0.21875 to 0.21875
- ln_gain_mlp: float32 [768], replicated, may hold values from 0.5 to 1.5
- w_up: bfloat16 [768, 3072], P('slide'), may hold values from -0.21875 to 0.21875
- w_down: bfloat16 [3072, 768], P('slide'), may hold values from -0.109375 to 0.109375
Outputs:
- encoded: bfloat16 [65536, 768], P(('slide', 'ctx'))
Inputs may be any that keep to these rules, and one draw needn't show every extreme that they name: `tile_slot`: over all devices every row number 0 to 65535 appears exactly once; the entries on each device include exactly 4 rows of the block of 512 rows of each device, devices ordered by slide and then ctx. `lengths`: some slide has exactly 4096 tiles.
All inputs are finite; a program needn't handle non-finite values.
Results may differ from a plain program's by a relative error of at most 0.009.
Values may be sent and summed in bfloat16 or wider, within the bound.
A program may use at most 256 MiB of HBM per device.

v0:
```python
import jax
import jax.numpy as jnp
from jax import lax
from jax.sharding import PartitionSpec as P

HEAD_DIM = 64


norm_eps = 1e-05
masked_score = -1e30


def from_behind(array, axis, by):
    peers = lax.axis_size(axis)
    return lax.ppermute(array, axis, [(i, (i + by) % peers) for i in range(peers)])


def layer_norm(rows, gain):
    values32 = rows.astype(jnp.float32)
    row_mean = jnp.mean(values32, axis=-1, keepdims=True)
    centred = values32 - row_mean
    row_var = jnp.mean(centred * centred, axis=-1, keepdims=True)
    return (centred * lax.rsqrt(row_var + norm_eps) * gain).astype(jnp.bfloat16)


def add_product(left_rows, piece):
    return jnp.dot(left_rows, piece, preferred_element_type=jnp.float32)


def empty_state(head_count, block_rows):
    return (
        jnp.full((head_count, block_rows), masked_score, jnp.float32),
        jnp.zeros((head_count, block_rows), jnp.float32),
        jnp.zeros((head_count, block_rows, HEAD_DIM), jnp.float32),
    )


def attend_rows(carry_state, queries, keyval, key_start, length):
    head_count = queries.shape[1]
    grouped = keyval.reshape(keyval.shape[0], 2, head_count, HEAD_DIM)
    scores = jnp.einsum(
        "qhd,khd->hqk", queries, grouped[:, 0], preferred_element_type=jnp.float32
    ) * HEAD_DIM ** (-0.5)
    key_pos = key_start + jnp.arange(keyval.shape[0], dtype=jnp.int32)
    scores = jnp.where(key_pos[None, None, :] < length, scores, masked_score)
    run_max, run_total, run_acc = carry_state
    new_max = jnp.maximum(run_max, jnp.max(scores, axis=-1))
    factor = jnp.exp(run_max - new_max)
    weights = jnp.exp(scores - new_max[:, :, None])
    new_total = run_total * factor + jnp.sum(weights, axis=-1)
    product = jnp.einsum(
        "hqk,khd->hqd",
        weights.astype(jnp.bfloat16),
        grouped[:, 1],
        preferred_element_type=jnp.float32,
    )
    return (new_max, new_total, run_acc * factor[:, :, None] + product)


def guarded(carry_state, queries, keyval, key_start, length):
    return attend_rows(carry_state, queries, keyval, key_start, length)


def finish(carry_state):
    run_max, run_total, run_acc = carry_state
    safe_total = jnp.where(run_total > 0.0, run_total, 1.0)
    result = run_acc / safe_total[:, :, None]
    head_count, block_rows, head_dim = result.shape
    return (
        jnp.transpose(result, (1, 0, 2))
        .reshape(block_rows, head_count * head_dim)
        .astype(jnp.bfloat16)
    )


def on_device(
    tile_rows, tile_slot, lengths, ln_gain_attn, w_query, w_kv, w_out, ln_gain_mlp, w_up, w_down
):
    block_rows, model_width = tile_rows.shape
    device_count = lax.axis_size(("slide", "ctx"))
    pair_rows = block_rows // device_count
    slot_ids = tile_slot[0]
    owners = slot_ids // block_rows
    ordering = jnp.argsort(owners, stable=True)
    outgoing = tile_rows[ordering].reshape(device_count, pair_rows, model_width)
    outgoing_slots = slot_ids[ordering].reshape(device_count, pair_rows)
    arrived, arrived_slots = (
        lax.all_to_all(outgoing, ("slide", "ctx"), split_axis=0, concat_axis=0, tiled=True),
        lax.all_to_all(outgoing_slots, ("slide", "ctx"), split_axis=0, concat_axis=0, tiled=True),
    )
    placing = jnp.argsort(arrived_slots.reshape(block_rows) % block_rows)
    tokens = arrived.reshape(block_rows, model_width)[placing]
    length = lengths[0]
    ctx_count = lax.axis_size("ctx")
    ctx_rank = lax.axis_index("ctx")
    query_start = ctx_rank * block_rows
    head_count = model_width // HEAD_DIM
    normed = layer_norm(tokens, ln_gain_attn)
    query_sum = add_product(normed, lax.all_gather(w_query, "slide", axis=0, tiled=True))
    keyval_sum = add_product(normed, lax.all_gather(w_kv, "slide", axis=0, tiled=True))
    moving = keyval_sum.astype(jnp.bfloat16)
    queries = query_sum.astype(jnp.bfloat16).reshape(block_rows, head_count, HEAD_DIM)
    carry_state = empty_state(head_count, block_rows)
    for turn_index in range(ctx_count):
        if turn_index > 0:
            moving = from_behind(moving, "ctx", 1)
        source = (ctx_rank - turn_index) % ctx_count
        carry_state = guarded(carry_state, queries, moving, source * block_rows, length)
    attended = finish(carry_state)
    out_sum = add_product(attended, lax.all_gather(w_out, "slide", axis=0, tiled=True))
    mid = (tokens.astype(jnp.float32) + out_sum).astype(jnp.bfloat16)
    normed_mlp = layer_norm(mid, ln_gain_mlp)
    up_sum = add_product(normed_mlp, lax.all_gather(w_up, "slide", axis=0, tiled=True))
    hidden = jax.nn.gelu(up_sum).astype(jnp.bfloat16)
    down_sum = add_product(hidden, lax.all_gather(w_down, "slide", axis=0, tiled=True))
    encoded = mid.astype(jnp.float32) + down_sum
    valid_rows = query_start + jnp.arange(block_rows, dtype=jnp.int32) < length
    return jnp.where(valid_rows[:, None], encoded, 0.0).astype(jnp.bfloat16)


def solution(mesh):
    return jax.shard_map(
        on_device,
        mesh=mesh,
        in_specs=(
            P(("slide", "ctx"), None),
            P(("slide", "ctx"), None),
            P("slide"),
            P(),
            P("slide", None),
            P("slide", None),
            P("slide", None),
            P(),
            P("slide", None),
            P("slide", None),
        ),
        out_specs=P(("slide", "ctx"), None),
        check_vma=False,
    )
```

profile of v0, /device:TPU:1, one launch (start us, length us, event | category | flops | bytes accessed | tf_op | source)
XLA Modules:
  0.0 472.3 jit_solution(14390095682409260824)
XLA Ops:
  10.0 3.8 sort.34
  13.8 3.6 gather_fusion.1
  18.1 11.5 %all-to-all-start.1 = ((s32[128,1,4]{2,1,0:T(1,128)}), s32[128,1,4]{2,1,0:T(1,128)S(1)}, u32[]{:S(2)}, u32[]{:S(2)}) async-start(s32[128,1,4]{2,1,0:T(1,128)} %bitcast.2), calls=%async_computation.1 | async-start | bytes 131072 | tf_op jit(solution)/shard_map/all_to_all | solution.py:89
  29.7 2.0 gather_fusion
  32.8 6.3 %all-to-all-done.1 = s32[128,1,4]{2,1,0:T(1,128)S(1)} async-done(((s32[128,1,4]{2,1,0:T(1,128)}), s32[128,1,4]{2,1,0:T(1,128)S(1)}, u32[]{:S(2)}, u32[]{:S(2)}) %all-to-all-start.1) | async-done | bytes 2080 | tf_op jit(solution)/shard_map/all_to_all | solution.py:89
  39.1 4.7 all-to-all-start
  45.2 3.7 sort.35
  49.0 12.2 %all-to-all-done = bf16[128,4,768]{2,1,0:T(4,128)(2,1)S(1)} async-done(((bf16[128,4,768]{2,1,0:T(4,128)(2,1)}), bf16[128,4,768]{2,1,0:T(4,128)(2,1)S(1)}, u32[]{:S(2)}, u32[]{:S(2)}) %all-to-all-start) | async-done | bytes 786464 | tf_op jit(solution)/shard_map/all_to_all | solution.py:88
  61.3 2.0 gather_fusion.2
  63.9 7.6 %all-gather.8.cloned.1.call-done = bf16[768,1536]{1,0:T(8,128)(2,1)} async-done(((bf16[48,1536]{1,0:T(8,128)(2,1)}), bf16[768,1536]{1,0:T(8,128)(2,1)}) %all-gather.8.cloned.1.call-update) | async-done | bytes 2359312 | tf_op jit(solution)/shard_map/all_gather | solution.py:100
  71.5 3.1 convolution_convert_fusion
  75.1 37.5 %collective-permute-done = bf16[512,1536]{1,0:T(8,128)(2,1)S(1)} collective-permute-done((bf16[512,1536]{1,0:T(8,128)(2,1)S(1)}, bf16[512,1536]{1,0:T(8,128)(2,1)S(1)}, u32[]{:S(2)}, u32[]{:S(2)}) %collective-permute-start) | collective-permute-done | bytes 1572896 | tf_op jit(solution)/shard_map/ppermute | solution.py:15
  112.6 36.9 %collective-permute-done.1 = bf16[512,1536]{1,0:T(8,128)(2,1)S(1)} collective-permute-done((bf16[512,1536]{1,0:T(8,128)(2,1)S(1)}, bf16[512,1536]{1,0:T(8,128)(2,1)S(1)}, u32[]{:S(2)}, u32[]{:S(2)}) %collective-permute-start.1) | collective-permute-done | bytes 1572896 | tf_op jit(solution)/shard_map/ppermute | solution.py:15
  152.1 34.5 %collective-permute-done.2 = bf16[512,1536]{1,0:T(8,128)(2,1)S(1)} collective-permute-done((bf16[512,1536]{1,0:T(8,128)(2,1)S(1)}, bf16[512,1536]{1,0:T(8,128)(2,1)S(1)}, u32[]{:S(2)}, u32[]{:S(2)}) %collective-permute-start.2) | collective-permute-done | bytes 1572896 | tf_op jit(solution)/shard_map/ppermute | solution.py:15
  188.0 33.8 %collective-permute-done.3 = bf16[512,1536]{1,0:T(8,128)(2,1)} collective-permute-done((bf16[512,1536]{1,0:T(8,128)(2,1)S(1)}, bf16[512,1536]{1,0:T(8,128)(2,1)}, u32[]{:S(2)}, u32[]{:S(2)}) %collective-permute-start.3) | collective-permute-done | bytes 1572896 | tf_op jit(solution)/shard_map/ppermute | solution.py:15
  221.7 2.2 collective-permute-start.4
  224.1 3.0 convolution_convert_fusion.1
  230.2 6.0 %fusion = (f32[12,512]{1,0:T(8,128)S(1)}, f32[12,512,512]{1,2,0:T(8,128)}) fusion(pred[512]{0:T(512)(128)(4,1)S(1)} %add_compare_fusion.7, bf16[512,12,64]{0,2,1:T(8,128)(2,1)S(1)} %bitcast.267, bf16[512,2,12,64]{0,3,2,1:T(8,128)(2,1)S(1)} %bitcast.281), kind=kOutput, calls=%fused_computation.19 | convolution fusion | flops 412084224 | bytes 14180864 | tf_op jit(solution)/shard_map/qhd,khd->hqk/dot_general | solution.py:41
  236.2 2.6 copy.64
  238.8 17.4 %collective-permute-done.4 = bf16[512,1536]{1,0:T(8,128)(2,1)} collective-permute-done((bf16[512,1536]{1,0:T(8,128)(2,1)}, bf16[512,1536]{1,0:T(8,128)(2,1)}, u32[]{:S(2)}, u32[]{:S(2)}) %collective-permute-start.4) | collective-permute-done | bytes 1572896 | tf_op jit(solution)/shard_map/ppermute | solution.py:15
  256.7 8.5 %fusion.1 = (f32[12,512]{1,0:T(8,128)S(1)}, f32[12,512,512]{1,2,0:T(8,128)}) fusion(pred[512]{0:T(512)(128)(4,1)S(1)} %add_compare_fusion.6, bf16[512,12,64]{0,2,1:T(8,128)(2,1)S(1)} %bitcast.268, bf16[512,2,12,64]{0,3,2,1:T(8,128)(2,1)} %bitcast.283), kind=kOutput, calls=%fused_computation.20 | convolution fusion | flops 412084224 | bytes 14180864 | tf_op jit(solution)/shard_map/qhd,khd->hqk/dot_general | solution.py:41
  265.1 2.6 copy.66
  267.7 8.5 %fusion.2 = (f32[12,512]{1,0:T(8,128)S(1)}, f32[12,512,512]{1,2,0:T(8,128)}) fusion(pred[512]{0:T(512)(128)(4,1)S(1)} %add_compare_fusion.5, bf16[512,12,64]{0,2,1:T(8,128)(2,1)S(1)} %bitcast.269, bf16[512,2,12,64]{0,3,2,1:T(8,128)(2,1)} %bitcast.285), kind=kOutput, calls=%fused_computation.21 | convolution fusion | flops 412084224 | bytes 14180864 | tf_op jit(solution)/shard_map/qhd,khd->hqk/dot_general | solution.py:41
  276.3 2.6 copy.68
  278.9 8.5 %fusion.3 = (f32[12,512]{1,0:T(8,128)S(1)}, f32[12,512,512]{1,2,0:T(8,128)}) fusion(pred[512]{0:T(512)(128)(4,1)S(1)} %add_compare_fusion.4, bf16[512,12,64]{0,2,1:T(8,128)(2,1)S(1)} %bitcast.270, bf16[512,2,12,64]{0,3,2,1:T(8,128)(2,1)} %bitcast.287), kind=kOutput, calls=%fused_computation.22 | convolution fusion | flops 412084224 | bytes 14180864 | tf_op jit(solution)/shard_map/qhd,khd->hqk/dot_general | solution.py:41
  287.3 2.6 copy.70
  291.6 8.4 %fusion.4 = (f32[12,512]{1,0:T(8,128)S(1)}, f32[12,512,512]{1,2,0:T(8,128)}) fusion(pred[512]{0:T(512)(128)(4,1)S(1)} %add_compare_fusion.3, bf16[512,12,64]{0,2,1:T(8,128)(2,1)S(1)} %bitcast.271, bf16[512,2,12,64]{0,3,2,1:T(8,128)(2,1)} %bitcast.289), kind=kOutput, calls=%fused_computation.23 | convolution fusion | flops 412084224 | bytes 14180864 | tf_op jit(solution)/shard_map/qhd,khd->hqk/dot_general | solution.py:41
  300.0 2.6 copy.72
  302.6 8.5 %fusion.5 = (f32[12,512]{1,0:T(8,128)S(1)}, f32[12,512,512]{1,2,0:T(8,128)}) fusion(pred[512]{0:T(512)(128)(4,1)S(1)} %add_compare_fusion.2, bf16[512,12,64]{0,2,1:T(8,128)(2,1)S(1)} %bitcast.272, bf16[512,2,12,64]{0,3,2,1:T(8,128)(2,1)} %bitcast.293), kind=kOutput, calls=%fused_computation.24 | convolution fusion | flops 412084224 | bytes 14180864 | tf_op jit(solution)/shard_map/qhd,khd->hqk/dot_general | solution.py:41
  311.1 2.6 copy.74
  313.7 8.5 %fusion.6 = (f32[12,512]{1,0:T(8,128)S(1)}, f32[12,512,512]{1,2,0:T(8,128)}) fusion(pred[512]{0:T(512)(128)(4,1)S(1)} %add_compare_fusion.1, bf16[512,12,64]{0,2,1:T(8,128)(2,1)S(1)} %bitcast.273, bf16[512,2,12,64]{0,3,2,1:T(8,128)(2,1)} %bitcast.295), kind=kOutput, calls=%fused_computation.25 | convolution fusion | flops 412084224 | bytes 14180864 | tf_op jit(solution)/shard_map/qhd,khd->hqk/dot_general | solution.py:41
  323.0 2.6 copy.76
  325.6 4.0 fusion.7
  329.7 12.8 %fusion.20 = (f32[12,512]{1,0:T(8,128)S(1)}, f32[12,512]{1,0:T(8,128)S(1)}) fusion(f32[12,512,512]{1,2,0:T(8,128)} %get-tuple-element.31, f32[12,512]{1,0:T(8,128)S(1)} %get-tuple-element.19, pred[512]{0:T(512)(128)(4,1)S(1)} %add_compare_fusion.1, f32[12,512]{1,0:T(8,128)S(1)} %get-tuple-element.18, f32[12,512,512]{1,2,0:T(8,128)S(1)} %get-tuple-element.29, ...), kind=kLoop, calls=%fused_computation.39 | loop fusion | flops 25153536 | bytes 25265152 | tf_op jit(solution)/shard_map/reduce_sum | solution.py:50
  342.6 9.4 %fusion.16 = (f32[12,512]{1,0:T(8,128)S(1)}, f32[12,512]{1,0:T(8,128)S(1)}) fusion(f32[12,512,512]{1,2,0:T(8,128)S(1)} %bitcast.280, f32[12,512]{1,0:T(8,128)S(1)} %get-tuple-element.21, pred[512]{0:T(512)(128)(4,1)S(1)} %add_compare_fusion.3, f32[12,512]{1,0:T(8,128)S(1)} %get-tuple-element.20, f32[12,512,512]{1,2,0:T(8,128)} %get-tuple-element.33, ...), kind=kLoop, calls=%fused_computation.35 | loop fusion | flops 25153536 | bytes 25265152 | tf_op jit(solution)/shard_map/reduce_sum | solution.py:50
  352.0 11.7 %fusion.12 = (f32[12,512]{1,0:T(8,128)S(1)}, f32[12,512]{1,0:T(8,128)S(1)}) fusion(f32[12,512,512]{1,2,0:T(8,128)} %get-tuple-element.39, f32[12,512]{1,0:T(8,128)S(1)} %get-tuple-element.23, pred[512]{0:T(512)(128)(4,1)S(1)} %add_compare_fusion.5, f32[12,512]{1,0:T(8,128)S(1)} %get-tuple-element.22, f32[12,512,512]{1,2,0:T(8,128)} %get-tuple-element.37, ...), kind=kLoop, calls=%fused_computation.31 | loop fusion | flops 25153536 | bytes 25265152 | tf_op jit(solution)/shard_map/reduce_sum | solution.py:50
  365.2 6.0 %fusion.8 = (f32[12,512]{1,0:T(8,128)S(1)}, f32[12,512]{1,0:T(8,128)S(1)}) fusion(f32[12,512,512]{1,2,0:T(8,128)S(1)} %bitcast.276, f32[12,512]{1,0:T(8,128)S(1)} %get-tuple-element.27, pred[512]{0:T(512)(128)(4,1)S(1)} %add_compare_fusion.7, f32[12,512]{1,0:T(8,128)S(1)} %get-tuple-element.24, f32[12,512,512]{1,2,0:T(8,128)S(1)} %bitcast.278, ...), kind=kLoop, calls=%fused_computation.27 | loop fusion | flops 25153536 | bytes 25265152 | tf_op jit(solution)/shard_map/reduce_sum | solution.py:50
  371.3 6.2 %fusion.34 = f32[12,512,64]{1,2,0:T(8,128)S(1)} fusion(f32[12,512,512]{1,2,0:T(8,128)} %get-tuple-element.31, f32[12,512]{1,0:T(8,128)S(1)} %get-tuple-element.19, pred[512]{0:T(512)(128)(4,1)S(1)} %add_compare_fusion.1, bf16[512,2,12,64]{0,3,2,1:T(8,128)(2,1)S(1)} %bitcast.296), kind=kOutput, calls=%fused_computation.53 | convolution fusion | flops 415236096 | bytes 14975488 | tf_op jit(solution)/shard_map/hqk,khd->hqd/dot_general | solution.py:51
  377.6 7.6 %fusion.36 = f32[12,512,64]{1,2,0:T(8,128)} fusion(f32[12,512,512]{1,2,0:T(8,128)} %get-tuple-element.33, f32[12,512]{1,0:T(8,128)S(1)} %get-tuple-element.20, pred[512]{0:T(512)(128)(4,1)S(1)} %add_compare_fusion.2, bf16[512,2,12,64]{0,3,2,1:T(8,128)(2,1)S(1)} %bitcast.294), kind=kOutput, calls=%fused_computation.54 | convolution fusion | flops 415236096 | bytes 14975488 | tf_op jit(solution)/shard_map/hqk,khd->hqd/dot_general | solution.py:51
  385.1 7.6 %fusion.38 = f32[12,512,64]{1,2,0:T(8,128)} fusion(f32[12,512,512]{1,2,0:T(8,128)} %get-tuple-element.35, f32[12,512]{1,0:T(8,128)S(1)} %get-tuple-element.21, pred[512]{0:T(512)(128)(4,1)S(1)} %add_compare_fusion.3, bf16[512,2,12,64]{0,3,2,1:T(8,128)(2,1)S(1)} %bitcast.290), kind=kOutput, calls=%fused_computation.55 | convolution fusion | flops 415236096 | bytes 14975488 | tf_op jit(solution)/shard_map/hqk,khd->hqd/dot_general | solution.py:51
  392.8 7.5 %fusion.40 = f32[12,512,64]{1,2,0:T(8,128)} fusion(f32[12,512,512]{1,2,0:T(8,128)} %get-tuple-element.37, f32[12,512]{1,0:T(8,128)S(1)} %get-tuple-element.22, pred[512]{0:T(512)(128)(4,1)S(1)} %add_compare_fusion.4, bf16[512,2,12,64]{0,3,2,1:T(8,128)(2,1)S(1)} %bitcast.288), kind=kOutput, calls=%fused_computation.56 | convolution fusion | flops 415236096 | bytes 14975488 | tf_op jit(solution)/shard_map/hqk,khd->hqd/dot_general | solution.py:51
  400.3 7.6 %fusion.42 = f32[12,512,64]{1,2,0:T(8,128)} fusion(f32[12,512,512]{1,2,0:T(8,128)} %get-tuple-element.39, f32[12,512]{1,0:T(8,128)S(1)} %get-tuple-element.23, pred[512]{0:T(512)(128)(4,1)S(1)} %add_compare_fusion.5, bf16[512,2,12,64]{0,3,2,1:T(8,128)(2,1)S(1)} %bitcast.286), kind=kOutput, calls=%fused_computation.57 | convolution fusion | flops 415236096 | bytes 14975488 | tf_op jit(solution)/shard_map/hqk,khd->hqd/dot_general | solution.py:51
  407.9 4.0 fusion.44
  411.9 4.0 fusion.46
  416.0 9.7 %fusion.72 = bf16[512,12,64]{0,2,1:T(8,128)(2,1)S(1)} fusion(f32[12,512,64]{1,2,0:T(8,128)S(1)} %fusion.34, f32[12,512,64]{1,2,0:T(8,128)S(1)} %copy-done.16, f32[12,512,64]{1,2,0:T(8,128)} %fusion.38, f32[12,512,64]{1,2,0:T(8,128)} %fusion.40, f32[12,512,64]{1,2,0:T(8,128)} %fusion.42, f32[12,512,64]{1,2,0:T(8,128)} %fusion.44, ...), kind=kOutput, calls=%fused_computation.91 | convolution fusion | flops 421920768 | bytes 25494016 | tf_op jit(solution)/shard_map/hqk,khd->hqd/dot_general | solution.py:51
  425.6 2.2 convert_reduce_fusion
  428.2 27.2 %all-gather.12.cloned.1.call-done = bf16[768,3072]{1,0:T(8,128)(2,1)} async-done(((bf16[48,3072]{1,0:T(8,128)(2,1)}), bf16[768,3072]{1,0:T(8,128)(2,1)}) %all-gather.12.cloned.1.call-update) | async-done | bytes 4718608 | tf_op jit(solution)/shard_map/all_gather | solution.py:113
  455.4 10.1 %fusion.70 = bf16[512,768]{1,0:T(8,128)(2,1)} fusion(bf16[512,768]{1,0:T(8,128)(2,1)S(1)} %get-tuple-element.45, bf16[3072,768]{1,0:T(8,128)(2,1)} %all-gather.14.cloned.1.call-done, bf16[768,3072]{1,0:T(8,128)(2,1)} %all-gather.12.cloned.1.call-done, f32[768]{0:T(1024)S(1)} %copy-done.15, f32[512]{0:T(512)S(1)} %add_rsqrt_fusion, ...), kind=kOutput, calls=%fused_computation.88 | convolution fusion | flops 4849532928 | bytes 11017728 | tf_op jit(solution)/shard_map/dot_general | solution.py:27
  (111 shorter events, 19.2 us)
Async XLA Ops:
  6.5 23.1 %copy-start = (bf16[512,768]{1,0:T(8,128)(2,1)S(1)}, bf16[512,768]{1,0:T(8,128)(2,1)}, u32[]{:S(2)}) copy-start(bf16[512,768]{1,0:T(8,128)(2,1)} %param.10) | copy-start | bytes 2359300
  6.5 64.9 %all-gather.8.cloned.1.call-start = ((), (), s32[]{:S(2)}) async-start(), calls=%async_computation.3 | async-start | bytes 2506752 | tf_op jit(solution)/shard_map/all_gather | solution.py:100
  7.3 216.8 %all-gather.6.cloned.1.call-start = ((), (), s32[]{:S(2)}) async-start(), calls=%async_computation.2 | async-start | bytes 1253376 | tf_op jit(solution)/shard_map/all_gather | solution.py:99
  8.0 417.6 %all-gather.10.cloned.1.call-start = ((), (), s32[]{:S(2)}) async-start(), calls=%async_computation.4 | async-start | bytes 1253376 | tf_op jit(solution)/shard_map/all_gather | solution.py:110
  8.7 419.5 %all-gather.14.cloned.1.call-start = ((), (), s32[]{:S(2)}) async-start(), calls=%async_computation.6 | async-start | bytes 5013504 | tf_op jit(solution)/shard_map/all_gather | solution.py:115
  18.1 21.0 %all-to-all-start.1 = ((s32[128,1,4]{2,1,0:T(1,128)}), s32[128,1,4]{2,1,0:T(1,128)S(1)}, u32[]{:S(2)}, u32[]{:S(2)}) async-start(s32[128,1,4]{2,1,0:T(1,128)} %bitcast.2), calls=%async_computation.1 | async-start | bytes 131072 | tf_op jit(solution)/shard_map/all_to_all | solution.py:89
  32.8 38.7 %copy-start.14 = (f32[768]{0:T(1024)S(1)}, f32[768]{0:T(1024)}, u32[]{:S(2)}) copy-start(f32[768]{0:T(1024)} %param.13) | copy-start | bytes 9220
  39.1 22.0 %all-to-all-start = ((bf16[128,4,768]{2,1,0:T(4,128)(2,1)}), bf16[128,4,768]{2,1,0:T(4,128)(2,1)S(1)}, u32[]{:S(2)}, u32[]{:S(2)}) async-start(bf16[128,4,768]{2,1,0:T(4,128)(2,1)} %reshape.340), calls=%async_computation | async-start | bytes 1572864 | tf_op jit(solution)/shard_map/all_to_all | solution.py:88
  43.8 411.6 %all-gather.12.cloned.1.call-start = ((), (), s32[]{:S(2)}) async-start(), calls=%async_computation.5 | async-start | bytes 5013504 | tf_op jit(solution)/shard_map/all_gather | solution.py:113
  74.6 112.0 %copy-start.12 = (bf16[512,1536]{1,0:T(8,128)(2,1)}, bf16[512,1536]{1,0:T(8,128)(2,1)S(1)}, u32[]{:S(2)}) copy-start(bf16[512,1536]{1,0:T(8,128)(2,1)S(1)} %convolution_convert_fusion) | copy-start | bytes 4718596
  74.6 38.0 %collective-permute-start = (bf16[512,1536]{1,0:T(8,128)(2,1)S(1)}, bf16[512,1536]{1,0:T(8,128)(2,1)S(1)}, u32[]{:S(2)}, u32[]{:S(2)}) collective-permute-start(bf16[512,1536]{1,0:T(8,128)(2,1)S(1)} %convolution_convert_fusion), channel_id=1, source_target_pairs={{0,1},{1,2},{2,3},{3,4},{4,5},{5,6},{6,7},{7,0},{8,9},{9,10},{10,1... | collective-permute-start | bytes 4718600 | tf_op jit(solution)/shard_map/ppermute | solution.py:15
  112.6 74.0 %copy-start.13 = (bf16[512,1536]{1,0:T(8,128)(2,1)}, bf16[512,1536]{1,0:T(8,128)(2,1)S(1)}, u32[]{:S(2)}) copy-start(bf16[512,1536]{1,0:T(8,128)(2,1)S(1)} %collective-permute-done) | copy-start | bytes 4718596
  112.6 36.9 %collective-permute-start.1 = (bf16[512,1536]{1,0:T(8,128)(2,1)S(1)}, bf16[512,1536]{1,0:T(8,128)(2,1)S(1)}, u32[]{:S(2)}, u32[]{:S(2)}) collective-permute-start(bf16[512,1536]{1,0:T(8,128)(2,1)S(1)} %collective-permute-done), channel_id=1, source_target_pairs={{0,1},{1,2},{2,3},{3,4},{4,5},{5,6},{6,7},{7,0},{8,9},{9,10},{10,1... | collective-permute-start | bytes 4718600 | tf_op jit(solution)/shard_map/ppermute | solution.py:15
  149.5 1.2 copy-start.10
  150.7 35.9 %collective-permute-start.2 = (bf16[512,1536]{1,0:T(8,128)(2,1)S(1)}, bf16[512,1536]{1,0:T(8,128)(2,1)S(1)}, u32[]{:S(2)}, u32[]{:S(2)}) collective-permute-start(bf16[512,1536]{1,0:T(8,128)(2,1)S(1)} %collective-permute-done.1), channel_id=1, source_target_pairs={{0,1},{1,2},{2,3},{3,4},{4,5},{5,6},{6,7},{7,0},{8,9},{9,10},{10,1... | collective-permute-start | bytes 4718600 | tf_op jit(solution)/shard_map/ppermute | solution.py:15
  186.6 40.5 %copy-start.11 = (bf16[512,1536]{1,0:T(8,128)(2,1)}, bf16[512,1536]{1,0:T(8,128)(2,1)S(1)}, u32[]{:S(2)}) copy-start(bf16[512,1536]{1,0:T(8,128)(2,1)S(1)} %collective-permute-done.2) | copy-start | bytes 4718596
  186.6 35.1 %collective-permute-start.3 = (bf16[512,1536]{1,0:T(8,128)(2,1)S(1)}, bf16[512,1536]{1,0:T(8,128)(2,1)}, u32[]{:S(2)}, u32[]{:S(2)}) collective-permute-start(bf16[512,1536]{1,0:T(8,128)(2,1)S(1)} %collective-permute-done.2), channel_id=1, source_target_pairs={{0,1},{1,2},{2,3},{3,4},{4,5},{5,6},{6,7},{7,0},{8,9},{9,10},{10,1... | collective-permute-start | bytes 4718600 | tf_op jit(solution)/shard_map/ppermute | solution.py:15
  221.7 34.5 %collective-permute-start.4 = (bf16[512,1536]{1,0:T(8,128)(2,1)}, bf16[512,1536]{1,0:T(8,128)(2,1)}, u32[]{:S(2)}, u32[]{:S(2)}) collective-permute-start(bf16[512,1536]{1,0:T(8,128)(2,1)} %collective-permute-done.3), channel_id=1, source_target_pairs={{0,1},{1,2},{2,3},{3,4},{4,5},{5,6},{6,7},{7,0},{8,9},{9,10},{10,1... | collective-permute-start | bytes 4718600 | tf_op jit(solution)/shard_map/ppermute | solution.py:15
  256.2 33.7 %collective-permute-start.5 = (bf16[512,1536]{1,0:T(8,128)(2,1)}, bf16[512,1536]{1,0:T(8,128)(2,1)}, u32[]{:S(2)}, u32[]{:S(2)}) collective-permute-start(bf16[512,1536]{1,0:T(8,128)(2,1)} %collective-permute-done.4), channel_id=1, source_target_pairs={{0,1},{1,2},{2,3},{3,4},{4,5},{5,6},{6,7},{7,0},{8,9},{9,10},{10,1... | collective-permute-start | bytes 4718600 | tf_op jit(solution)/shard_map/ppermute | solution.py:15
  289.9 33.1 %collective-permute-start.6 = (bf16[512,1536]{1,0:T(8,128)(2,1)}, bf16[512,1536]{1,0:T(8,128)(2,1)}, u32[]{:S(2)}, u32[]{:S(2)}) collective-permute-start(bf16[512,1536]{1,0:T(8,128)(2,1)} %collective-permute-done.5), channel_id=1, source_target_pairs={{0,1},{1,2},{2,3},{3,4},{4,5},{5,6},{6,7},{7,0},{8,9},{9,10},{10,1... | collective-permute-start | bytes 4718600 | tf_op jit(solution)/shard_map/ppermute | solution.py:15
  329.6 12.9 %copy-start.2 = (f32[12,512,512]{1,2,0:T(8,128)}, f32[12,512,512]{1,2,0:T(8,128)S(1)}, u32[]{:S(2)}) copy-start(f32[12,512,512]{1,2,0:T(8,128)S(1)} %get-tuple-element.29) | copy-start | bytes 37748740
  329.6 12.9 %slice-start.6 = ((s8[12582912]{0:T(1024)(128)(4,1)}), s8[4194304]{0:T(1024)(128)(4,1)S(1)}, s32[]{:S(2)}) async-start(s8[12582912]{0:T(1024)(128)(4,1)} %bitcast.279), calls=%async_computation.13 | async-start | bytes 8388608
  329.6 12.9 %slice-start.7 = ((s8[12582912]{0:T(1024)(128)(4,1)}), s8[4194304]{0:T(1024)(128)(4,1)S(1)}, s32[]{:S(2)}) async-start(s8[12582912]{0:T(1024)(128)(4,1)} %bitcast.279), calls=%async_computation.14 | async-start | bytes 8388608
  329.7 12.9 %slice-start.8 = ((s8[12582912]{0:T(1024)(128)(4,1)}), s8[4194304]{0:T(1024)(128)(4,1)S(1)}, s32[]{:S(2)}) async-start(s8[12582912]{0:T(1024)(128)(4,1)} %bitcast.279), calls=%async_computation.15 | async-start | bytes 8388608
  342.6 21.1 %slice-start.3 = ((s8[12582912]{0:T(1024)(128)(4,1)}), s8[4194304]{0:T(1024)(128)(4,1)S(1)}, s32[]{:S(2)}) async-start(s8[12582912]{0:T(1024)(128)(4,1)} %bitcast.277), calls=%async_computation.10 | async-start | bytes 8388608
  342.6 21.1 %slice-start.4 = ((s8[12582912]{0:T(1024)(128)(4,1)}), s8[4194304]{0:T(1024)(128)(4,1)S(1)}, s32[]{:S(2)}) async-start(s8[12582912]{0:T(1024)(128)(4,1)} %bitcast.277), calls=%async_computation.11 | async-start | bytes 8388608
  352.0 11.7 %slice-start = ((s8[12582912]{0:T(1024)(128)(4,1)}), s8[4194304]{0:T(1024)(128)(4,1)S(1)}, s32[]{:S(2)}) async-start(s8[12582912]{0:T(1024)(128)(4,1)} %bitcast.275), calls=%async_computation.7 | async-start | bytes 8388608
  352.0 11.7 %slice-start.1 = ((s8[12582912]{0:T(1024)(128)(4,1)}), s8[4194304]{0:T(1024)(128)(4,1)S(1)}, s32[]{:S(2)}) async-start(s8[12582912]{0:T(1024)(128)(4,1)} %bitcast.275), calls=%async_computation.8 | async-start | bytes 8388608
  352.0 12.0 %slice-start.2 = ((s8[12582912]{0:T(1024)(128)(4,1)}), s8[4194304]{0:T(1024)(128)(4,1)S(1)}, s32[]{:S(2)}) async-start(s8[12582912]{0:T(1024)(128)(4,1)} %bitcast.275), calls=%async_computation.9 | async-start | bytes 8388608
  352.0 13.2 %slice-start.5 = ((s8[12582912]{0:T(1024)(128)(4,1)}), s8[4194304]{0:T(1024)(128)(4,1)S(1)}, s32[]{:S(2)}) async-start(s8[12582912]{0:T(1024)(128)(4,1)} %bitcast.277), calls=%async_computation.12 | async-start | bytes 8388608
  365.2 6.1 %copy-start.9 = (bf16[512,1536]{0,1:T(8,128)(2,1)S(1)}, bf16[512,1536]{0,1:T(8,128)(2,1)}, u32[]{:S(2)}) copy-start(bf16[512,1536]{0,1:T(8,128)(2,1)} %copy.74) | copy-start | bytes 4718596
  371.3 6.3 %copy-start.8 = (bf16[512,1536]{0,1:T(8,128)(2,1)S(1)}, bf16[512,1536]{0,1:T(8,128)(2,1)}, u32[]{:S(2)}) copy-start(bf16[512,1536]{0,1:T(8,128)(2,1)} %copy.72) | copy-start | bytes 4718596
  377.6 7.6 %copy-start.6 = (bf16[512,1536]{0,1:T(8,128)(2,1)S(1)}, bf16[512,1536]{0,1:T(8,128)(2,1)}, u32[]{:S(2)}) copy-start(bf16[512,1536]{0,1:T(8,128)(2,1)} %copy.70) | copy-start | bytes 4718596
  385.1 7.6 %copy-start.5 = (bf16[512,1536]{0,1:T(8,128)(2,1)S(1)}, bf16[512,1536]{0,1:T(8,128)(2,1)}, u32[]{:S(2)}) copy-start(bf16[512,1536]{0,1:T(8,128)(2,1)} %copy.68) | copy-start | bytes 4718596
  392.8 7.5 %copy-start.4 = (bf16[512,1536]{0,1:T(8,128)(2,1)S(1)}, bf16[512,1536]{0,1:T(8,128)(2,1)}, u32[]{:S(2)}) copy-start(bf16[512,1536]{0,1:T(8,128)(2,1)} %copy.66) | copy-start | bytes 4718596
  400.3 7.6 %copy-start.3 = (bf16[512,1536]{0,1:T(8,128)(2,1)S(1)}, bf16[512,1536]{0,1:T(8,128)(2,1)}, u32[]{:S(2)}) copy-start(bf16[512,1536]{0,1:T(8,128)(2,1)} %copy.64) | copy-start | bytes 4718596
  411.9 4.0 copy-start.7
  411.9 4.0 copy-start.16
  416.0 39.5 %copy-start.15 = (f32[768]{0:T(1024)S(1)}, f32[768]{0:T(1024)}, u32[]{:S(2)}) copy-start(f32[768]{0:T(1024)} %param.17) | copy-start | bytes 9220
  455.4 10.1 %copy-start.1 = (bf16[512,768]{1,0:T(8,128)(2,1)S(1)}, bf16[512,768]{1,0:T(8,128)(2,1)}, u32[]{:S(2)}) copy-start(bf16[512,768]{1,0:T(8,128)(2,1)} %param.10) | copy-start | bytes 2359300
Sparse Core Ops, SparseCore 0:
  9.8 61.6 all-gather.7
  73.9 73.4 all-gather.5
  149.9 72.4 all-gather.9
  224.7 171.7 all-gather.13
  398.8 56.5 all-gather.11
where the time goes:
time: 480 us; the launch traced here: 472 us
  waiting for transfers between devices  217 us (45%)
  matrix products  134 us (28%)
  other arithmetic  50 us (10%)
  local copies, waits for them, and re-layouts  34.2 us (7%)
  starting transfers between devices  23.2 us (5%)
  between operations  14.6 us (3%)
    ppermute x7, waiting for transfers between devices, from_behind(): lax.ppermute(array, axis, [(i, (i + by) % peers) for i in range(peers)])  161 us
    dot_general x8, matrix products, attend_rows(): jnp.einsum('qhd,khd->hqk', queries, grouped[:, 0], preferred_element_type...  60.9 us
    dot_general x8, matrix products, attend_rows(): jnp.einsum('hqk,khd->hqd', weights.astype(jnp.bfloat16), grouped[:, 1], p...  54.2 us
    reduce_sum x4, other arithmetic, attend_rows(): new_total = run_total * factor + jnp.sum(weights, axis=-1)  39.9 us
    all_gather x1, waiting for transfers between devices, on_device(): lax.all_gather(w_up, 'slide', axis=0, tiled=True)  27.2 us
    dot_general x4, matrix products, add_product(): return jnp.dot(left_rows, piece, preferred_element_type=jnp.float32)  18.4 us
    ppermute x7, local copies, waits for them, and re-layouts, from_behind(): lax.ppermute(array, axis, [(i, (i + by) % peers) for i in range(peers)])  18.1 us
    all_to_all x1, waiting for transfers between devices, on_device(): lax.all_to_all(outgoing, ('slide', 'ctx'), split_axis=0, concat_axis=0, t...  12.2 us
  transfers between devices with their start and end apart: 14, of which 10 were waited for; matrix products, arithmetic and copies ran while one was open for 43% of the time, Pallas kernels for 0%

commit v1 on v0

v1 whole, which is shorter than its diff:
```python
import functools

import jax
import jax.numpy as jnp
from jax import lax
from jax.experimental import pallas as pl
from jax.experimental.pallas import tpu as pltpu
from jax.sharding import PartitionSpec as P

HEAD_DIM = 64
MESH = pl.DeviceIdType.MESH
bf16, f32 = jnp.bfloat16, jnp.float32

norm_eps = 1e-05
masked_score = -1e30
value_rows = 80
ORDER = [
    (0, 0), (0, 1), (1, 0), (2, 0), (3, 0), (1, 1), (2, 1), (3, 1),
    (6, 0), (5, 0), (6, 1), (4, 0), (7, 0), (4, 1), (5, 1), (7, 1),
]


def layer_norm(rows, gain):
    values32 = rows.astype(f32)
    row_mean = jnp.mean(values32, axis=-1, keepdims=True)
    centred = values32 - row_mean
    row_var = jnp.mean(centred * centred, axis=-1, keepdims=True)
    return (centred * lax.rsqrt(row_var + norm_eps) * gain).astype(bf16)


def dot(left, right):
    return jnp.dot(left, right, preferred_element_type=f32)


def dot_nt(left, right):
    return lax.dot_general(left, right, (((1,), (1,)), ((), ())), preferred_element_type=f32)


def identity(size):
    row = lax.broadcasted_iota(jnp.int32, (size, size), 0)
    column = lax.broadcasted_iota(jnp.int32, (size, size), 1)
    return jnp.where(row == column, 1.0, 0.0).astype(bf16)


def layer_kernel(
    tok, length_ref, gain1, wq, wkv, wo, gain2, wu, wd,
    out,
    rows, w_a, w_b, w_c, w_vt, q_aug, k_buf, v_buf, bias, scores, top, acc, attended, up_buf, down_acc,
    t_send, t_recv, a_send, a_recv, b_send, b_recv, c_send, c_recv,
):
    block, width = tok.shape
    half = block // 2
    heads = width // HEAD_DIM
    pairs = heads // 2
    hidden = wu.shape[1]
    slide = lax.axis_index("slide")
    ctx = lax.axis_index("ctx")
    z_hi, x, core = lax.div(slide, 8), lax.rem(lax.div(slide, 2), 4), lax.rem(slide, 2)
    y, z_lo = lax.div(ctx, 2), lax.rem(ctx, 2)

    def at_slide(zz, xx, cc):
        return zz * 8 + lax.rem(xx + 4, 4) * 2 + cc

    def at_ctx(yy, zz):
        return lax.rem(yy + 4, 4) * 2 + zz

    y_next = (slide, at_ctx(y + 1, z_lo))
    y_prev = (slide, at_ctx(y - 1, z_lo))
    z_pair = (slide, at_ctx(y, 1 - z_lo))
    x_next = (at_slide(z_hi, x + 1, core), ctx)
    x_prev = (at_slide(z_hi, x - 1, core), ctx)
    zw_pair = (at_slide(1 - z_hi, x, core), at_ctx(y, 1 - z_lo))
    sibling = (at_slide(z_hi, x, 1 - core), ctx)

    barrier = pltpu.get_barrier_semaphore()
    for peer in (y_next, y_prev, z_pair, x_next, x_prev, zw_pair, sibling):
        pl.semaphore_signal(barrier, inc=1, device_id=peer, device_id_type=MESH)
    pl.semaphore_wait(barrier, 7)

    def shard_of(relation, cc):
        zz = (1 - z_hi) if relation in (3, 4, 5, 7) else z_hi
        step = {0: 0, 1: -1, 2: 1, 3: 0, 4: -1, 5: 1, 6: 2, 7: 2}[relation]
        return at_slide(zz, x + step, cc)

    class Gather:
        def __init__(self, whole, depth, send, recv):
            self.whole, self.depth, self.send, self.recv = whole, depth, send, recv
            self.started = []

        def part(self, relation, cc, side=None):
            at = pl.ds(pl.multiple_of(shard_of(relation, cc) * self.depth, 16), self.depth)
            if side is None:
                return self.whole.at[at, :]
            cut = self.whole.shape[1] // 2
            return self.whole.at[at, pl.ds(side * cut, cut)]

        def handle(self, key, send_slot, slot, peer):
            part = self.part(*key)
            return pltpu.make_async_remote_copy(
                src_ref=part, dst_ref=part, send_sem=self.send.at[send_slot],
                recv_sem=self.recv.at[slot], device_id=peer, device_id_type=MESH,
            )

        def copy(self, key, peer, slot):
            self.handle(key, len(self.started), slot, peer).start()
            self.started.append(key)

        def arrive(self, key, slot):
            self.handle(key, 0, slot, sibling).wait_recv()

        def first(self):
            own = (0, core)
            self.copy(own, x_next, 1)
            self.copy(own, x_prev, 2)
            self.copy(own, zw_pair, 3)
            self.copy(own, sibling, 8)

        def second(self):
            for relation in (1, 2, 3):
                self.arrive((relation, core), relation)
            self.copy((1, core, 0), x_next, 6)
            self.copy((2, core, 1), x_prev, 0)
            self.copy((3, core), x_next, 4)
            self.copy((3, core), x_prev, 5)
            for relation in (1, 2, 3):
                self.copy((relation, core), sibling, 8 + relation)

        def third(self):
            self.arrive((6, core, 0), 6)
            self.arrive((6, core, 1), 0)
            self.copy((6, core), zw_pair, 7)
            self.copy((6, core), sibling, 14)

        def fourth(self):
            for relation in (4, 5, 7):
                self.arrive((relation, core), relation)
                self.copy((relation, core), sibling, 8 + relation)

        def last(self):
            for relation in range(8):
                self.arrive((relation, 1 - core), 8 + relation)

        def sent(self):
            for index, key in enumerate(self.started):
                self.handle(key, index, 0, sibling).wait_send()

    gather_a = Gather(w_a, wq.shape[0], a_send, a_recv)
    gather_b = Gather(w_b, wu.shape[0], b_send, b_recv)
    gather_c = Gather(w_c, wd.shape[0], c_send, c_recv)

    own48 = pl.ds(pl.multiple_of(slide * wq.shape[0], 16), wq.shape[0])
    w_a[own48, 0:width] = wq[...]
    w_a[own48, width:] = wkv[...]
    gather_a.first()

    place = {key: index for index, key in enumerate(ORDER)}

    def chunk(relation, side):
        return rows.at[pl.ds(place[relation, side] * half, half), :]

    token_sends = []

    def rows_handle(source, target, send_slot, peer):
        return pltpu.make_async_remote_copy(
            src_ref=chunk(*source), dst_ref=chunk(*target), send_sem=t_send.at[send_slot],
            recv_sem=t_recv.at[place[target]], device_id=peer, device_id_type=MESH,
        )

    def pass_rows(source, relation, side, peer):
        rows_handle(source, (relation, side), len(token_sends), peer).start()
        token_sends.append(source)

    def rows_here(relation, side):
        rows_handle((relation, side), (relation, side), 0, sibling).wait_recv()

    for side in range(2):
        rows[side * half : (side + 1) * half, :] = layer_norm(
            tok[side * half : (side + 1) * half, :], gain1[...]
        )
        pass_rows((0, side), 1, side, y_next)
        pass_rows((0, side), 2, side, y_prev)
        pass_rows((0, side), 3, side, z_pair)

    w_b[own48, 0:width] = wo[...]
    w_b[own48, width:] = wu[...]
    own192 = pl.ds(pl.multiple_of(slide * wd.shape[0], 16), wd.shape[0])
    w_c[own192, :] = wd[...]

    q_aug[...] = jnp.zeros(q_aug.shape, bf16)
    q_aug[:, 128:144, :] = jnp.where(
        lax.broadcasted_iota(jnp.int32, (pairs, 16, 2 * block), 1) == 0, 1.0, 0.0
    ).astype(bf16)
    v_buf[:, 64:80, :] = jnp.where(
        lax.broadcasted_iota(jnp.int32, (heads, 16, block), 1) == 0, 1.0, 0.0
    ).astype(bf16)
    top[...] = jnp.full(top.shape, masked_score, f32)
    acc[...] = jnp.zeros(acc.shape, f32)

    gather_a.second()
    gather_a.third()
    for relation in (1, 2, 3):
        rows_here(relation, 0)
    pass_rows((1, 0), 6, 0, y_next)
    pass_rows((3, 0), 5, 0, y_prev)
    pass_rows((3, 0), 4, 0, y_next)
    gather_a.fourth()
    gather_b.first()
    gather_a.last()

    scale = HEAD_DIM ** (-0.5) * 1.4426950408889634
    queries = (dot(rows[0:block, :], w_a[:, 0:width]) * scale).astype(bf16)
    queries_t = dot_nt(identity(width), queries).astype(bf16)
    for head in range(heads):
        pair, at = head // 2, head % 2
        q_aug[pair, at * 64 : at * 64 + 64, at * block : (at + 1) * block] = queries_t[
            head * 64 : head * 64 + 64, :
        ]
    w_vt[...] = dot_nt(identity(width), w_a[:, 2 * width :]).astype(bf16)

    length = length_ref[0]

    def position(relation, side):
        step = {0: 0, 1: -1, 2: 1, 3: 0, 4: -1, 5: 1, 6: 2, 7: 2}[relation]
        zz = (1 - z_lo) if relation in (3, 4, 5, 7) else z_lo
        return at_ctx(y + step, zz) * block + side * half

    def attend(step, first, second):
        here = rows[pl.ds(pl.multiple_of(step * block, block), block), :]
        k_buf[...] = dot(here, w_a[:, width : 2 * width]).astype(bf16)
        values_t = dot_nt(w_vt[...], here).astype(bf16)
        for head in range(heads):
            v_buf[head, 0:64, :] = values_t[head * 64 : head * 64 + 64, :]
        line = lax.broadcasted_iota(jnp.int32, (block, 128), 0)
        lane = lax.broadcasted_iota(jnp.int32, (block, 128), 1)
        at = jnp.where(line < half, first + line, second + line - half)
        bias[...] = jnp.where((lane == 0) & (at >= length), masked_score, 0.0).astype(bf16)

        def score(pair, slot):
            keys = k_buf[:, pl.ds(pl.multiple_of(pair * 128, 128), 128)]
            scores[slot] = dot(jnp.concatenate([keys, bias[...]], axis=1), q_aug[pair])

        def soften(pair, slot):
            before = top[pair]
            now = jnp.maximum(before, jnp.max(scores[slot], axis=0, keepdims=True))
            factor = jnp.exp2(before - now)
            top[pair] = now
            for side in range(2):
                span = slice(side * block, (side + 1) * block)
                weights = jnp.exp2(scores[slot, :, span] - now[:, span]).astype(bf16)
                head = 2 * pair + side
                acc[head] = acc[head] * factor[:, span] + dot(v_buf[head], weights)

        score(0, 0)

        def two(index, _):
            score(2 * index + 1, 1)
            soften(2 * index, 0)
            score(jnp.minimum(2 * index + 2, pairs - 1), 0)
            soften(2 * index + 1, 1)
            return 0

        lax.fori_loop(0, pairs // 2, two, 0)

    steps = len(ORDER) // 2
    firsts = [position(*ORDER[2 * step]) for step in range(steps)]
    seconds = [position(*ORDER[2 * step + 1]) for step in range(steps)]

    def pick(options, step):
        chosen = options[0]
        for index in range(1, len(options)):
            chosen = jnp.where(step == index, options[index], chosen)
        return chosen

    def turn(step, _):
        @pl.when(step == 2)
        def _():
            for relation in (1, 2, 3):
                rows_here(relation, 1)
            pass_rows((3, 1), 4, 1, y_next)
            pass_rows((2, 1), 6, 1, y_prev)
            pass_rows((3, 1), 5, 1, y_prev)
            gather_b.second()

        @pl.when(step == 3)
        def _():
            gather_b.third()
            gather_c.first()

        @pl.when(step == 4)
        def _():
            rows_here(6, 0)
            pass_rows((6, 0), 7, 0, z_pair)
            rows_here(5, 0)
            gather_b.fourth()

        @pl.when(step == 5)
        def _():
            rows_here(6, 1)
            pass_rows((6, 1), 7, 1, z_pair)
            rows_here(4, 0)
            gather_c.second()

        @pl.when(step == 6)
        def _():
            rows_here(7, 0)
            rows_here(4, 1)
            gather_c.third()

        @pl.when(step == 7)
        def _():
            rows_here(5, 1)
            rows_here(7, 1)
            gather_c.fourth()

        attend(step, pick(firsts, step), pick(seconds, step))
        return 0

    lax.fori_loop(0, steps, turn, 0)

    gather_b.last()
    for head in range(heads):
        done = acc[head]
        attended[head * 64 : head * 64 + 64, :] = (done[0:64] / done[64:65]).astype(bf16)
    turned = dot_nt(identity(block), attended[...]).astype(bf16)
    mid = (tok[...].astype(f32) + dot(turned, w_b[:, 0:width])).astype(bf16)
    for index, source in enumerate(token_sends):
        rows_handle(source, source, index, sibling).wait_send()
    rows[0:block, :] = layer_norm(mid, gain2[...])
    gather_c.last()
    down_acc[...] = mid.astype(f32)

    tile = up_buf.shape[2]
    tiles = hidden // tile

    def up(index, slot):
        at = pl.ds(pl.multiple_of(width + index * tile, 128), tile)
        up_buf[slot] = dot(rows[0:block, :], w_b[:, at])

    def down(index, slot):
        active = jax.nn.gelu(up_buf[slot], approximate=True).astype(bf16)
        down_acc[...] += dot(active, w_c[pl.ds(pl.multiple_of(index * tile, tile), tile), :])

    up(0, 0)

    def two_tiles(index, _):
        up(2 * index + 1, 1)
        down(2 * index, 0)
        up(jnp.minimum(2 * index + 2, tiles - 1), 0)
        down(2 * index + 1, 1)
        return 0

    lax.fori_loop(0, tiles // 2, two_tiles, 0)
    at = ctx * block + lax.broadcasted_iota(jnp.int32, (block, width), 0)
    out[...] = jnp.where(at < length, down_acc[...], 0.0).astype(bf16)

    for gather in (gather_a, gather_b, gather_c):
        gather.sent()


def layer(tokens, lengths, gain1, wq, wkv, wo, gain2, wu, wd):
    block, width = tokens.shape
    heads = width // HEAD_DIM
    hidden = wu.shape[1]
    slides = lax.axis_size("slide")
    vmem = pl.BlockSpec(memory_space=pltpu.VMEM)
    dma = pltpu.SemaphoreType.DMA
    return pl.pallas_call(
        layer_kernel,
        out_shape=jax.ShapeDtypeStruct((block, width), bf16),
        in_specs=[vmem, pl.BlockSpec(memory_space=pltpu.SMEM)] + [vmem] * 7,
        out_specs=vmem,
        scratch_shapes=[
            pltpu.VMEM((8 * block, width), bf16),
            pltpu.VMEM((width, 3 * width), bf16),
            pltpu.VMEM((width, width + hidden), bf16),
            pltpu.VMEM((hidden, width), bf16),
            pltpu.VMEM((width, width), bf16),
            pltpu.VMEM((heads // 2, 256, 2 * block), bf16),
            pltpu.VMEM((block, width), bf16),
            pltpu.VMEM((heads, value_rows, block), bf16),
            pltpu.VMEM((block, 128), bf16),
            pltpu.VMEM((2, block, 2 * block), f32),
            pltpu.VMEM((heads // 2, 1, 2 * block), f32),
            pltpu.VMEM((heads, value_rows, block), f32),
            pltpu.VMEM((width, block), bf16),
            pltpu.VMEM((2, block, 512), f32),
            pltpu.VMEM((block, width), f32),
            dma((14,)), dma((16,)),
            dma((16,)), dma((16,)),
            dma((16,)), dma((16,)),
            dma((16,)), dma((16,)),
        ],
        compiler_params=pltpu.CompilerParams(
            collective_id=0, has_side_effects=True, vmem_limit_bytes=60 * 2**20
        ),
        name="layer",
    )(tokens, lengths, gain1.reshape(1, width), wq, wkv, wo, gain2.reshape(1, width), wu, wd)


def on_device(
    tile_rows, tile_slot, lengths, ln_gain_attn, w_query, w_kv, w_out, ln_gain_mlp, w_up, w_down
):
    block_rows, model_width = tile_rows.shape
    device_count = lax.axis_size(("slide", "ctx"))
    pair_rows = block_rows // device_count
    slot_ids = tile_slot[0]
    owners = slot_ids // block_rows
    ordering = jnp.argsort(owners, stable=True)
    outgoing = tile_rows[ordering].reshape(device_count, pair_rows, model_width)
    outgoing_slots = slot_ids[ordering].reshape(device_count, pair_rows)
    arrived, arrived_slots = (
        lax.all_to_all(outgoing, ("slide", "ctx"), split_axis=0, concat_axis=0, tiled=True),
        lax.all_to_all(outgoing_slots, ("slide", "ctx"), split_axis=0, concat_axis=0, tiled=True),
    )
    placing = jnp.argsort(arrived_slots.reshape(block_rows) % block_rows)
    tokens = arrived.reshape(block_rows, model_width)[placing]
    return layer(tokens, lengths, ln_gain_attn, w_query, w_kv, w_out, ln_gain_mlp, w_up, w_down)


def solution(mesh):
    return jax.shard_map(
        on_device,
        mesh=mesh,
        in_specs=(
            P(("slide", "ctx"), None),
            P(("slide", "ctx"), None),
            P("slide"),
            P(),
            P("slide", None),
            P("slide", None),
            P("slide", None),
            P(),
            P("slide", None),
            P("slide", None),
        ),
        out_specs=P(("slide", "ctx"), None),
        check_vma=False,
    )
```

time: 480 us -> 146 us (0.30); the launches traced: 472 us -> 146 us
  waiting for transfers between devices: 217 us -> 14.7 us
  matrix products: 134 us -> 0 us
  Pallas kernels: 0 us -> 90.1 us
  other arithmetic: 50 us -> 9.2 us
  local copies, waits for them, and re-layouts: 34.2 us -> 14.9 us
  between operations: 14.6 us -> 0.75 us
  starting transfers between devices: 23.2 us -> 16.2 us
    ppermute x7 -> x0, waiting for transfers between devices: 161 us -> none  [from_behind(): lax.ppermute(array, axis, [(i, (i + by) % peers) for i in range(peers)])]
    dot_general x20 -> x0, matrix products: 134 us -> none  [the longest x8 60.9 us: attend_rows(): jnp.einsum('qhd,khd->hqk', queries, grouped[:, 0], preferred_element_type...]
    pallas_call x0 -> x1, Pallas kernels: none -> 90.1 us  [layer(): pl.pallas_call(layer_kernel, out_shape=jax.ShapeDtypeStruct((block, width...]
    reduce_sum x7 -> x0, other arithmetic: 40.8 us -> none  [the longest x4 39.9 us: attend_rows(): new_total = run_total * factor + jnp.sum(weights, axis=-1)]
    all_gather x5 -> x0, waiting for transfers between devices: 34.8 us -> none  [the longest x1 27.2 us: on_device(): lax.all_gather(w_up, 'slide', axis=0, tiled=True)]
    ppermute x7 -> x0, local copies, waits for them, and re-layouts: 18.1 us -> none  [from_behind(): lax.ppermute(array, axis, [(i, (i + by) % peers) for i in range(peers)])]
    ppermute x7 -> x0, starting transfers between devices: 6.81 us -> none  [from_behind(): lax.ppermute(array, axis, [(i, (i + by) % peers) for i in range(peers)])]
  transfers between devices with their start and end apart: 14 -> 2, of which waited for: 10 -> 2; matrix products, arithmetic and copies ran while one was open for 43% -> 7% of each run, Pallas kernels for 0% -> 0%
where the time goes in v1:
time: 146 us
  Pallas kernels  90.1 us (62%)
  starting transfers between devices  16.2 us (11%)
  local copies, waits for them, and re-layouts  14.9 us (10%)
  waiting for transfers between devices  14.7 us (10%)
  other arithmetic  9.2 us (6%)
    pallas_call x1, Pallas kernels, layer(): pl.pallas_call(layer_kernel, out_shape=jax.ShapeDtypeStruct((block, width...  90.1 us
    all_to_all x1, starting transfers between devices, on_device(): lax.all_to_all(outgoing_slots, ('slide', 'ctx'), split_axis=0, concat_axi...  11.5 us
    all_to_all x1, waiting for transfers between devices, on_device(): lax.all_to_all(outgoing, ('slide', 'ctx'), split_axis=0, concat_axis=0, t...  8.38 us
    all_to_all x1, waiting for transfers between devices, on_device(): lax.all_to_all(outgoing_slots, ('slide', 'ctx'), split_axis=0, concat_axi...  6.34 us
    all_to_all x1, starting transfers between devices, on_device(): lax.all_to_all(outgoing, ('slide', 'ctx'), split_axis=0, concat_axis=0, t...  4.7 us
    sort x1, other arithmetic, on_device(): placing = jnp.argsort(arrived_slots.reshape(block_rows) % block_rows)  3.78 us
    sort x1, other arithmetic, on_device(): ordering = jnp.argsort(owners, stable=True)  3.77 us
    gather x1, local copies, waits for them, and re-layouts, on_device(): outgoing_slots = slot_ids[ordering].reshape(device_count, pair_rows)  3.48 us
  transfers between devices with their start and end apart: 2, of which 2 were waited for; matrix products, arithmetic and copies ran while one was open for 7% of the time, Pallas kernels for 0%

profile of v1, /device:TPU:1, one launch (start us, length us, event | category | flops | bytes accessed | tf_op | source)
XLA Modules:
  0.0 145.9 jit_solution(8669137688521919705)
XLA Ops:
  0.0 0.0 copy-start
  0.0 0.8 add_select_fusion.1
  0.8 3.8 %sort.34 = (s32[512]{0:T(512)}, s32[512]{0:T(512)S(1)}) sort(s32[512]{0:T(512)S(1)} %add_select_fusion.1, s32[512]{0:T(512)S(1)} %iota.8), dimensions={0}, to_apply=%region_0.1 | sort | flops 4608 | bytes 8192 | tf_op jit(solution)/shard_map/jit(argsort)/sort | solution.py:408
  4.5 0.0 copy-start.1
  4.6 0.7 copy-done.1
  5.2 3.5 %gather_fusion.1 = s32[512]{0:T(512)S(1)} fusion(s32[512]{0:T(512)S(1)} %bitcast.3, s32[1024]{0:T(1024)S(1)} %pad_clamp_fusion.1), kind=kCustom, calls=%fused_computation.1 | custom fusion | bytes 6144 | tf_op jit(solution)/shard_map/gather | solution.py:410
  8.7 0.7 all_to_all.10
  9.4 11.5 %all-to-all-start.1 = ((s32[128,1,4]{2,1,0:T(1,128)}), s32[128,1,4]{2,1,0:T(1,128)S(1)}, u32[]{:S(2)}, u32[]{:S(2)}) async-start(s32[128,1,4]{2,1,0:T(1,128)} %bitcast.1), calls=%async_computation.1 | async-start | bytes 131072 | tf_op jit(solution)/shard_map/all_to_all | solution.py:413
  20.9 0.0 copy-done
  21.0 2.0 %gather_fusion = bf16[512,768]{1,0:T(8,128)(2,1)S(1)} fusion(bf16[512,768]{1,0:T(8,128)(2,1)S(1)} %copy-done, s32[1024]{0:T(1024)S(1)} %pad_clamp_fusion.1), kind=kCustom, calls=%fused_computation | custom fusion | bytes 1574912 | tf_op jit(solution)/shard_map/gather | solution.py:409
  23.0 1.1 reshape.20
  24.0 0.0 copy-start.2
  24.1 6.3 %all-to-all-done.1 = s32[128,1,4]{2,1,0:T(1,128)S(1)} async-done(((s32[128,1,4]{2,1,0:T(1,128)}), s32[128,1,4]{2,1,0:T(1,128)S(1)}, u32[]{:S(2)}, u32[]{:S(2)}) %all-to-all-start.1) | async-done | bytes 2080 | tf_op jit(solution)/shard_map/all_to_all | solution.py:413
  30.4 4.7 %all-to-all-start = ((bf16[128,4,768]{2,1,0:T(4,128)(2,1)}), bf16[128,4,768]{2,1,0:T(4,128)(2,1)S(1)}, u32[]{:S(2)}, u32[]{:S(2)}) async-start(bf16[128,4,768]{2,1,0:T(4,128)(2,1)} %reshape.20), calls=%async_computation | async-start | bytes 1572864 | tf_op jit(solution)/shard_map/all_to_all | solution.py:412
  35.1 0.0 copy-done.2
  35.1 0.0 copy-start.3
  35.1 0.6 reshape.23.gain1
  35.7 0.1 copy-done.3
  35.8 0.6 reshape.24.gain2
  37.0 0.6 broadcast.31
  37.6 0.8 reduce.3
  38.5 0.1 reshape.22
  38.6 3.8 %sort.35 = (s32[512]{0:T(512)}, s32[512]{0:T(512)S(1)}) sort(s32[512]{0:T(512)S(1)} %add_select_fusion, s32[512]{0:T(512)S(1)} %iota.9), dimensions={0}, to_apply=%region_1.2 | sort | flops 4608 | bytes 8192 | tf_op jit(solution)/shard_map/jit(argsort)/sort | solution.py:415
  42.4 8.4 %all-to-all-done = bf16[128,4,768]{2,1,0:T(4,128)(2,1)S(1)} async-done(((bf16[128,4,768]{2,1,0:T(4,128)(2,1)}), bf16[128,4,768]{2,1,0:T(4,128)(2,1)S(1)}, u32[]{:S(2)}, u32[]{:S(2)}) %all-to-all-start) | async-done | bytes 786464 | tf_op jit(solution)/shard_map/all_to_all | solution.py:412
  50.8 0.2 reshape.21
  51.0 2.7 %gather_fusion.2 = bf16[512,768]{1,0:T(8,128)(2,1)} fusion(bf16[512,768]{1,0:T(8,128)(2,1)S(1)} %reshape.21, s32[1024]{0:T(1024)S(1)} %pad_clamp_fusion), kind=kCustom, calls=%fused_computation.2 | custom fusion | bytes 1574912 | tf_op jit(solution)/shard_map/gather | solution.py:416
  53.7 90.1 %layer.1 = bf16[512,768]{1,0:T(8,128)(2,1)} custom-call(bf16[512,768]{1,0:T(8,128)(2,1)} %gather_fusion.2, s32[1]{0:T(128)S(6)} %copy.13.length_ref, f32[1,768]{1,0:T(1,128)} %reshape.23.gain1, bf16[48,768]{1,0:T(8,128)(2,1)} %wq.1, bf16[48,1536]{1,0:T(8,128)(2,1)} %wkv.1, bf16[48,768]{1,0:T(8,128)(2,1)} %wo.1, f32[1,768]{1,0:T(1,128)} %reshape.24.gain2, ...), custom_call_target="tpu_custom_call" | custom-call | tf_op jit(solution)/shard_map/layer/pallas_call | solution.py:367
  143.8 2.1 %copy.14 = bf16[512,768]{1,0:T(8,128)(2,1)} copy(bf16[512,768]{1,0:T(8,128)(2,1)} %layer.1) | data formatting | bytes 1572864
  (7 shorter events, 0.0 us)
Async XLA Ops:
  0.0 20.9 %copy-start = (bf16[512,768]{1,0:T(8,128)(2,1)S(1)}, bf16[512,768]{1,0:T(8,128)(2,1)}, u32[]{:S(2)}) copy-start(bf16[512,768]{1,0:T(8,128)(2,1)} %param.10) | copy-start | bytes 2359300
  4.5 0.7 copy-start.1
  9.4 20.9 %all-to-all-start.1 = ((s32[128,1,4]{2,1,0:T(1,128)}), s32[128,1,4]{2,1,0:T(1,128)S(1)}, u32[]{:S(2)}, u32[]{:S(2)}) async-start(s32[128,1,4]{2,1,0:T(1,128)} %bitcast.1), calls=%async_computation.1 | async-start | bytes 131072 | tf_op jit(solution)/shard_map/all_to_all | solution.py:413
  24.0 11.1 %copy-start.2 = (f32[768]{0:T(1024)S(1)}, f32[768]{0:T(1024)}, u32[]{:S(2)}) copy-start(f32[768]{0:T(1024)} %param.13) | copy-start | bytes 9220
  30.4 20.4 %all-to-all-start = ((bf16[128,4,768]{2,1,0:T(4,128)(2,1)}), bf16[128,4,768]{2,1,0:T(4,128)(2,1)S(1)}, u32[]{:S(2)}, u32[]{:S(2)}) async-start(bf16[128,4,768]{2,1,0:T(4,128)(2,1)} %reshape.20), calls=%async_computation | async-start | bytes 1572864 | tf_op jit(solution)/shard_map/all_to_all | solution.py:412
  35.1 0.7 copy-start.3

commit v2 on v1

--- a/solution.py
+++ b/solution.py
@@ -43,10 +43,11 @@
 
 
 def layer_kernel(
-    tok, length_ref, gain1, wq, wkv, wo, gain2, wu, wd,
+    tile_rows, tile_slot, length_ref, gain1, wq, wkv, wo, gain2, wu, wd,
     out,
+    outgoing, in_slide, by_ctx, in_block, tok, masks, eye,
     rows, w_a, w_b, w_c, w_vt, q_aug, k_buf, v_buf, bias, scores, top, acc, attended, up_buf, down_acc,
-    t_send, t_recv, a_send, a_recv, b_send, b_recv, c_send, c_recv,
+    s_send, s_recv, p_send, p_recv, m_send, m_recv, t_send, t_recv, a_send, a_recv, b_send, b_recv, c_send, c_recv,
 ):
     block, width = tok.shape
     half = block // 2
@@ -72,10 +73,13 @@
     zw_pair = (at_slide(1 - z_hi, x, core), at_ctx(y, 1 - z_lo))
     sibling = (at_slide(z_hi, x, 1 - core), ctx)
 
+    slides, ctxs = 16, 8
+    slide_peers = [(lax.rem(slide + by, slides), ctx) for by in range(1, slides)]
+    ctx_peers = [(slide, lax.rem(ctx + by, ctxs)) for by in range(1, ctxs)]
     barrier = pltpu.get_barrier_semaphore()
-    for peer in (y_next, y_prev, z_pair, x_next, x_prev, zw_pair, sibling):
+    for peer in slide_peers + ctx_peers + [zw_pair]:
         pl.semaphore_signal(barrier, inc=1, device_id=peer, device_id_type=MESH)
-    pl.semaphore_wait(barrier, 7)
+    pl.semaphore_wait(barrier, slides + ctxs - 1)
 
     def shard_of(relation, cc):
         zz = (1 - z_hi) if relation in (3, 4, 5, 7) else z_hi
@@ -153,6 +157,82 @@
     w_a[own48, width:] = wkv[...]
     gather_a.first()
 
+    def grid(shape, dim):
+        return lax.broadcasted_iota(jnp.int32, shape, dim)
+
+    slots = tile_slot[...]
+    devices = slides * ctxs
+    share = block // devices
+    owned = jnp.where((slots >> 9) == grid((devices, block), 0), 1.0, 0.0)
+    earlier = jnp.where(grid((block, block), 0) < grid((block, block), 1), 1.0, 0.0).astype(bf16)
+    ahead = dot(owned.astype(bf16), earlier)
+    first_row = (grid((devices, block), 0) * share).astype(f32)
+    target = jnp.sum(owned * (first_row + ahead), axis=0, keepdims=True)
+    sorting = jnp.where(grid((block, block), 0).astype(f32) == target, 1.0, 0.0).astype(bf16)
+    lane = grid((128, block), 0)
+    digits = jnp.where(lane == 0, (slots >> 6) & 63, jnp.where(lane == 1, slots & 63, 0))
+    outgoing[:, 0:width] = dot(sorting, tile_rows[...]).astype(bf16)
+    outgoing[:, width:] = dot_nt(sorting, digits.astype(f32).astype(bf16)).astype(bf16)
+
+    def pieces(buffer, index, depth):
+        return buffer.at[pl.ds(pl.multiple_of(index * depth, 16), depth), :]
+
+    def exchange(source, target, depth, me, count, peers, send, recv):
+        def handle(by, peer):
+            return pltpu.make_async_remote_copy(
+                src_ref=pieces(source, lax.rem(me + by, count), depth),
+                dst_ref=pieces(target, me, depth), send_sem=send.at[by],
+                recv_sem=recv.at[by], device_id=peer, device_id_type=MESH,
+            )
+
+        def incoming(by, peer):
+            part = pieces(target, lax.rem(me + count - by, count), depth)
+            return pltpu.make_async_remote_copy(
+                src_ref=part, dst_ref=part, send_sem=send.at[by],
+                recv_sem=recv.at[by], device_id=peer, device_id_type=MESH,
+            )
+
+        def start():
+            for by in range(1, count):
+                handle(by, peers[by - 1]).start()
+            at = pl.ds(pl.multiple_of(me * depth, 16), depth)
+            target[at, :] = source[at, :]
+
+        def arrive():
+            for by in range(1, count):
+                incoming(by, peers[by - 1]).wait_recv()
+
+        def sent():
+            for by in range(1, count):
+                handle(by, peers[by - 1]).wait_send()
+
+        return start, arrive, sent
+
+    slide_rows = block // slides
+    ctx_rows = block // ctxs
+    to_slides = exchange(outgoing, in_slide, slide_rows, slide, slides, slide_peers, s_send, s_recv)
+    to_blocks = exchange(by_ctx, in_block, ctx_rows, ctx, ctxs, ctx_peers, p_send, p_recv)
+    to_slides[0]()
+
+    w_b[own48, 0:width] = wo[...]
+    w_b[own48, width:] = wu[...]
+    own192 = pl.ds(pl.multiple_of(slide * wd.shape[0], 16), wd.shape[0])
+    w_c[own192, :] = wd[...]
+    eye[...] = identity(width)
+    q_aug[...] = jnp.zeros(q_aug.shape, bf16)
+    q_aug[:, 128:144, :] = jnp.where(grid((pairs, 16, 2 * block), 1) == 0, 1.0, 0.0).astype(bf16)
+    v_buf[:, 64:80, :] = jnp.where(grid((heads, 16, block), 1) == 0, 1.0, 0.0).astype(bf16)
+    top[...] = jnp.full(top.shape, masked_score, f32)
+    acc[...] = jnp.zeros(acc.shape, f32)
+    gather_a.second()
+
+    to_slides[1]()
+    wanted = grid((block, block), 0)
+    wanted = ((wanted >> 2) & 15) * slide_rows + (wanted >> 6) * share + (wanted & 3)
+    turning = jnp.where(grid((block, block), 1) == wanted, 1.0, 0.0).astype(bf16)
+    by_ctx[...] = dot(turning, in_slide[...]).astype(bf16)
+    to_blocks[0]()
+
     place = {key: index for index, key in enumerate(ORDER)}
 
     def chunk(relation, side):
@@ -174,66 +254,72 @@
         rows_handle((relation, side), (relation, side), 0, sibling).wait_recv()
 
     for side in range(2):
-        rows[side * half : (side + 1) * half, :] = layer_norm(
-            tok[side * half : (side + 1) * half, :], gain1[...]
-        )
+        part = slice(side * half, (side + 1) * half)
+        rows[part, :] = layer_norm(in_slide[part, 0:width], gain1[...])
         pass_rows((0, side), 1, side, y_next)
         pass_rows((0, side), 2, side, y_prev)
         pass_rows((0, side), 3, side, z_pair)
 
-    w_b[own48, 0:width] = wo[...]
-    w_b[own48, width:] = wu[...]
-    own192 = pl.ds(pl.multiple_of(slide * wd.shape[0], 16), wd.shape[0])
-    w_c[own192, :] = wd[...]
-
-    q_aug[...] = jnp.zeros(q_aug.shape, bf16)
-    q_aug[:, 128:144, :] = jnp.where(
-        lax.broadcasted_iota(jnp.int32, (pairs, 16, 2 * block), 1) == 0, 1.0, 0.0
-    ).astype(bf16)
-    v_buf[:, 64:80, :] = jnp.where(
-        lax.broadcasted_iota(jnp.int32, (heads, 16, block), 1) == 0, 1.0, 0.0
-    ).astype(bf16)
-    top[...] = jnp.full(top.shape, masked_score, f32)
-    acc[...] = jnp.zeros(acc.shape, f32)
-
-    gather_a.second()
+    def positions(buffer):
+        weight = grid((8, 128), 1)
+        weight = jnp.where(weight == 0, 64.0, jnp.where(weight == 1, 1.0, 0.0)).astype(bf16)
+        return dot_nt(weight, buffer[:, width:])
+
+    length = length_ref[0]
+    masked = jnp.where(positions(in_slide) >= length.astype(f32), masked_score, 0.0)
+    masks[ctx, 0] = masked[:, 0:half]
+    masks[ctx, 1] = masked[:, half:]
+
+    def mask_handle(by, owner):
+        return pltpu.make_async_remote_copy(
+            src_ref=masks.at[owner], dst_ref=masks.at[owner], send_sem=m_send.at[by],
+            recv_sem=m_recv.at[by], device_id=ctx_peers[by - 1], device_id_type=MESH,
+        )
+
+    for by in range(1, ctxs):
+        mask_handle(by, ctx).start()
+
     gather_a.third()
-    for relation in (1, 2, 3):
-        rows_here(relation, 0)
-    pass_rows((1, 0), 6, 0, y_next)
-    pass_rows((3, 0), 5, 0, y_prev)
-    pass_rows((3, 0), 4, 0, y_next)
     gather_a.fourth()
     gather_b.first()
     gather_a.last()
+    w_vt[...] = dot_nt(eye[...], w_a[:, 2 * width :]).astype(bf16)
+
+    def project(step):
+        here = rows[pl.ds(pl.multiple_of(step * block, block), block), :]
+        k_buf[...] = dot(here, w_a[:, width : 2 * width]).astype(bf16)
+        values_t = dot_nt(w_vt[...], here).astype(bf16)
+        for head in range(heads):
+            v_buf[head, 0:64, :] = values_t[head * 64 : head * 64 + 64, :]
+
+    project(0)
+
+    to_blocks[1]()
+    at_row = positions(in_block)[0:1] - (ctx * block).astype(f32)
+    placing = jnp.where(grid((block, block), 0).astype(f32) == at_row, 1.0, 0.0).astype(bf16)
+    tok[...] = dot(placing, in_block[:, 0:width]).astype(bf16)
 
     scale = HEAD_DIM ** (-0.5) * 1.4426950408889634
-    queries = (dot(rows[0:block, :], w_a[:, 0:width]) * scale).astype(bf16)
-    queries_t = dot_nt(identity(width), queries).astype(bf16)
+    queries = (dot(layer_norm(tok[...], gain1[...]), w_a[:, 0:width]) * scale).astype(bf16)
+    queries_t = dot_nt(eye[...], queries).astype(bf16)
     for head in range(heads):
         pair, at = head // 2, head % 2
         q_aug[pair, at * 64 : at * 64 + 64, at * block : (at + 1) * block] = queries_t[
             head * 64 : head * 64 + 64, :
         ]
-    w_vt[...] = dot_nt(identity(width), w_a[:, 2 * width :]).astype(bf16)
-
-    length = length_ref[0]
-
-    def position(relation, side):
+
+    for by in range(1, ctxs):
+        mask_handle(by, lax.rem(ctx + ctxs - by, ctxs)).wait_recv()
+
+    def owner(relation):
         step = {0: 0, 1: -1, 2: 1, 3: 0, 4: -1, 5: 1, 6: 2, 7: 2}[relation]
         zz = (1 - z_lo) if relation in (3, 4, 5, 7) else z_lo
-        return at_ctx(y + step, zz) * block + side * half
-
-    def attend(step, first, second):
-        here = rows[pl.ds(pl.multiple_of(step * block, block), block), :]
-        k_buf[...] = dot(here, w_a[:, width : 2 * width]).astype(bf16)
-        values_t = dot_nt(w_vt[...], here).astype(bf16)
-        for head in range(heads):
-            v_buf[head, 0:64, :] = values_t[head * 64 : head * 64 + 64, :]
-        line = lax.broadcasted_iota(jnp.int32, (block, 128), 0)
-        lane = lax.broadcasted_iota(jnp.int32, (block, 128), 1)
-        at = jnp.where(line < half, first + line, second + line - half)
-        bias[...] = jnp.where((lane == 0) & (at >= length), masked_score, 0.0).astype(bf16)
+        return at_ctx(y + step, zz)
+
+    def attend(first, first_side, second, second_side):
+        here = jnp.concatenate([masks[first, first_side], masks[second, second_side]], axis=1)
+        here = jnp.concatenate([here, jnp.zeros((120, block), f32)], axis=0).astype(bf16)
+        bias[...] = dot_nt(eye[0:block, 0:block], here).astype(bf16)
 
         def score(pair, slot):
             keys = k_buf[:, pl.ds(pl.multiple_of(pair * 128, 128), 128)]
@@ -262,8 +348,10 @@
         lax.fori_loop(0, pairs // 2, two, 0)
 
     steps = len(ORDER) // 2
-    firsts = [position(*ORDER[2 * step]) for step in range(steps)]
-    seconds = [position(*ORDER[2 * step + 1]) for step in range(steps)]
+    firsts = [owner(ORDER[2 * step][0]) for step in range(steps)]
+    seconds = [owner(ORDER[2 * step + 1][0]) for step in range(steps)]
+    first_sides = [ORDER[2 * step][1] for step in range(steps)]
+    second_sides = [ORDER[2 * step + 1][1] for step in range(steps)]
 
     def pick(options, step):
         chosen = options[0]
@@ -272,6 +360,14 @@
         return chosen
 
     def turn(step, _):
+        @pl.when(step == 1)
+        def _():
+            for relation in (1, 2, 3):
+                rows_here(relation, 0)
+            pass_rows((1, 0), 6, 0, y_next)
+            pass_rows((3, 0), 5, 0, y_prev)
+            pass_rows((3, 0), 4, 0, y_next)
+
         @pl.when(step == 2)
         def _():
             for relation in (1, 2, 3):
@@ -312,7 +408,13 @@
             rows_here(7, 1)
             gather_c.fourth()
 
-        attend(step, pick(firsts, step), pick(seconds, step))
+        @pl.when(step > 0)
+        def _():
+            project(step)
+
+        attend(
+            pick(firsts, step), pick(first_sides, step), pick(seconds, step), pick(second_sides, step)
+        )
         return 0
 
     lax.fori_loop(0, steps, turn, 0)
@@ -321,7 +423,7 @@
     for head in range(heads):
         done = acc[head]
         attended[head * 64 : head * 64 + 64, :] = (done[0:64] / done[64:65]).astype(bf16)
-    turned = dot_nt(identity(block), attended[...]).astype(bf16)
+    turned = dot_nt(eye[0:block, 0:block], attended[...]).astype(bf16)
     mid = (tok[...].astype(f32) + dot(turned, w_b[:, 0:width])).astype(bf16)
     for index, source in enumerate(token_sends):
         rows_handle(source, source, index, sibling).wait_send()
@@ -353,23 +455,35 @@
     at = ctx * block + lax.broadcasted_iota(jnp.int32, (block, width), 0)
     out[...] = jnp.where(at < length, down_acc[...], 0.0).astype(bf16)
 
+    to_slides[2]()
+    to_blocks[2]()
+    for by in range(1, ctxs):
+        mask_handle(by, ctx).wait_send()
     for gather in (gather_a, gather_b, gather_c):
         gather.sent()
 
 
-def layer(tokens, lengths, gain1, wq, wkv, wo, gain2, wu, wd):
-    block, width = tokens.shape
+def on_device(
+    tile_rows, tile_slot, lengths, ln_gain_attn, w_query, w_kv, w_out, ln_gain_mlp, w_up, w_down
+):
+    block, width = tile_rows.shape
     heads = width // HEAD_DIM
-    hidden = wu.shape[1]
-    slides = lax.axis_size("slide")
+    hidden = w_up.shape[1]
     vmem = pl.BlockSpec(memory_space=pltpu.VMEM)
     dma = pltpu.SemaphoreType.DMA
     return pl.pallas_call(
         layer_kernel,
         out_shape=jax.ShapeDtypeStruct((block, width), bf16),
-        in_specs=[vmem, pl.BlockSpec(memory_space=pltpu.SMEM)] + [vmem] * 7,
+        in_specs=[vmem, vmem, pl.BlockSpec(memory_space=pltpu.SMEM)] + [vmem] * 7,
         out_specs=vmem,
         scratch_shapes=[
+            pltpu.VMEM((block, width + 128), bf16),
+            pltpu.VMEM((block, width + 128), bf16),
+            pltpu.VMEM((block, width + 128), bf16),
+            pltpu.VMEM((block, width + 128), bf16),
+            pltpu.VMEM((block, width), bf16),
+            pltpu.VMEM((8, 2, 8, block // 2), f32),
+            pltpu.VMEM((width, width), bf16),
             pltpu.VMEM((8 * block, width), bf16),
             pltpu.VMEM((width, 3 * width), bf16),
             pltpu.VMEM((width, width + hidden), bf16),
@@ -385,6 +499,9 @@
             pltpu.VMEM((width, block), bf16),
             pltpu.VMEM((2, block, 512), f32),
             pltpu.VMEM((block, width), f32),
+            dma((16,)), dma((16,)),
+            dma((8,)), dma((8,)),
+            dma((8,)), dma((8,)),
             dma((14,)), dma((16,)),
             dma((16,)), dma((16,)),
             dma((16,)), dma((16,)),
@@ -394,27 +511,10 @@
             collective_id=0, has_side_effects=True, vmem_limit_bytes=60 * 2**20
         ),
         name="layer",
-    )(tokens, lengths, gain1.reshape(1, width), wq, wkv, wo, gain2.reshape(1, width), wu, wd)
-
-
-def on_device(
-    tile_rows, tile_slot, lengths, ln_gain_attn, w_query, w_kv, w_out, ln_gain_mlp, w_up, w_down
-):
-    block_rows, model_width = tile_rows.shape
-    device_count = lax.axis_size(("slide", "ctx"))
-    pair_rows = block_rows // device_count
-    slot_ids = tile_slot[0]
-    owners = slot_ids // block_rows
-    ordering = jnp.argsort(owners, stable=True)
-    outgoing = tile_rows[ordering].reshape(device_count, pair_rows, model_width)
-    outgoing_slots = slot_ids[ordering].reshape(device_count, pair_rows)
-    arrived, arrived_slots = (
-        lax.all_to_all(outgoing, ("slide", "ctx"), split_axis=0, concat_axis=0, tiled=True),
-        lax.all_to_all(outgoing_slots, ("slide", "ctx"), split_axis=0, concat_axis=0, tiled=True),
+    )(
+        tile_rows, tile_slot, lengths, ln_gain_attn.reshape(1, width), w_query, w_kv, w_out,
+        ln_gain_mlp.reshape(1, width), w_up, w_down,
     )
-    placing = jnp.argsort(arrived_slots.reshape(block_rows) % block_rows)
-    tokens = arrived.reshape(block_rows, model_width)[placing]
-    return layer(tokens, lengths, ln_gain_attn, w_query, w_kv, w_out, ln_gain_mlp, w_up, w_down)
 
 
 def solution(mesh):

time: 146 us -> 130 us (0.89); the launches traced: 146 us -> 128 us
  Pallas kernels: 90.1 us -> 123 us
  starting transfers between devices: 16.2 us -> 0 us
  waiting for transfers between devices: 14.7 us -> 0 us
  local copies, waits for them, and re-layouts: 14.9 us -> 3.93 us
  other arithmetic: 9.2 us -> 0 us
    pallas_call x1, Pallas kernels: 90.1 us -> 123 us  [on_device(): pl.pallas_call(layer_kernel, out_shape=jax.ShapeDtypeStruct((block, width...]
    all_to_all x2 -> x0, starting transfers between devices: 16.2 us -> none  [the longest x1 11.5 us: on_device(): lax.all_to_all(outgoing_slots, ('slide', 'ctx'), split_axis=0, concat_axi...]
    all_to_all x2 -> x0, waiting for transfers between devices: 14.7 us -> none  [the longest x1 8.38 us: on_device(): lax.all_to_all(outgoing, ('slide', 'ctx'), split_axis=0, concat_axis=0, t...]
    gather x3 -> x0, local copies, waits for them, and re-layouts: 8.22 us -> none  [the longest x1 3.48 us: on_device(): outgoing_slots = slot_ids[ordering].reshape(device_count, pair_rows)]
    sort x2 -> x0, other arithmetic: 7.55 us -> none  [the longest x1 3.78 us: on_device(): placing = jnp.argsort(arrived_slots.reshape(block_rows) % block_rows)]
  transfers between devices with their start and end apart: 2 -> 0, of which waited for: 2 -> 0; matrix products, arithmetic and copies ran while one was open for 7% -> 0% of each run, Pallas kernels for 0% -> 0%
where the time goes in v2:
time: 130 us; the launch traced here: 128 us
  Pallas kernels  123 us (95%)
  local copies, waits for them, and re-layouts  3.93 us (3%)
    pallas_call x1, Pallas kernels, on_device(): pl.pallas_call(layer_kernel, out_shape=jax.ShapeDtypeStruct((block, width...  123 us

profile of v2, /device:TPU:1, one launch (start us, length us, event | category | flops | bytes accessed | tf_op | source)
XLA Modules:
  0.0 128.0 jit_solution(11307982168886835786)
XLA Ops:
  0.0 0.0 copy-start
  0.7 1.3 reshape.6.gain1
  1.9 0.0 copy-done
  1.9 0.6 reshape.7.gain2
  2.5 123.4 %layer.1 = bf16[512,768]{1,0:T(8,128)(2,1)} custom-call(bf16[512,768]{1,0:T(8,128)(2,1)} %tile_rows.1, s32[1,512]{1,0:T(1,128)} %tile_slot.1, s32[1]{0:T(128)S(6)} %copy.12.length_ref, f32[1,768]{1,0:T(1,128)} %reshape.6.gain1, bf16[48,768]{1,0:T(8,128)(2,1)} %wq.1, bf16[48,1536]{1,0:T(8,128)(2,1)} %wkv.1, bf16[48,768]{1,0:T(8,128)(2,1)} %wo.1, ...), custom_call_target="tpu_custom_call" | custom-call | tf_op jit(solution)/shard_map/layer/pallas_call | solution.py:474
  126.0 2.1 %copy.13 = bf16[512,768]{1,0:T(8,128)(2,1)} copy(bf16[512,768]{1,0:T(8,128)(2,1)} %layer.1) | data formatting | bytes 1572864
Async XLA Ops:
  0.0 1.9 %copy-start = (f32[768]{0:T(1024)S(1)}, f32[768]{0:T(1024)}, u32[]{:S(2)}) copy-start(f32[768]{0:T(1024)} %param.17) | copy-start | bytes 9220

commit v3 on v2

--- a/solution.py
+++ b/solution.py
@@ -15,8 +15,8 @@
 masked_score = -1e30
 value_rows = 80
 ORDER = [
-    (0, 0), (0, 1), (1, 0), (2, 0), (3, 0), (1, 1), (2, 1), (3, 1),
-    (6, 0), (5, 0), (6, 1), (4, 0), (7, 0), (4, 1), (5, 1), (7, 1),
+    (0, 0), (0, 1), (4, 0), (4, 1), (1, 0), (2, 1), (5, 0), (6, 1),
+    (1, 1), (2, 0), (5, 1), (6, 0), (3, 0), (3, 1), (7, 0), (7, 1),
 ]
 
 
@@ -45,11 +45,11 @@
 def layer_kernel(
     tile_rows, tile_slot, length_ref, gain1, wq, wkv, wo, gain2, wu, wd,
     out,
-    outgoing, in_slide, by_ctx, in_block, tok, masks, eye,
+    outgoing, in_slide, by_ctx, finished, landed, lengths, masks, eye,
     rows, w_a, w_b, w_c, w_vt, q_aug, k_buf, v_buf, bias, scores, top, acc, attended, up_buf, down_acc,
-    s_send, s_recv, p_send, p_recv, m_send, m_recv, t_send, t_recv, a_send, a_recv, b_send, b_recv, c_send, c_recv,
+    s_send, s_recv, f_send, f_recv, m_send, m_recv, l_sem, t_send, t_recv, a_send, a_recv, b_send, b_recv, c_send, c_recv,
 ):
-    block, width = tok.shape
+    block, width = tile_rows.shape
     half = block // 2
     heads = width // HEAD_DIM
     pairs = heads // 2
@@ -65,21 +65,36 @@
     def at_ctx(yy, zz):
         return lax.rem(yy + 4, 4) * 2 + zz
 
+    slides, ctxs = 16, 8
     y_next = (slide, at_ctx(y + 1, z_lo))
     y_prev = (slide, at_ctx(y - 1, z_lo))
-    z_pair = (slide, at_ctx(y, 1 - z_lo))
     x_next = (at_slide(z_hi, x + 1, core), ctx)
     x_prev = (at_slide(z_hi, x - 1, core), ctx)
     zw_pair = (at_slide(1 - z_hi, x, core), at_ctx(y, 1 - z_lo))
     sibling = (at_slide(z_hi, x, 1 - core), ctx)
 
-    slides, ctxs = 16, 8
-    slide_peers = [(lax.rem(slide + by, slides), ctx) for by in range(1, slides)]
-    ctx_peers = [(slide, lax.rem(ctx + by, ctxs)) for by in range(1, ctxs)]
+    work = at_slide(z_hi, x, z_lo)
+    member = y * 2 + core
+
+    def works_on(index):
+        return (
+            at_slide(lax.div(index, 8), lax.rem(lax.div(index, 2), 4), core),
+            at_ctx(y, lax.rem(index, 2)),
+        )
+
+    def at_member(index):
+        return (at_slide(z_hi, x, lax.rem(index, 2)), at_ctx(lax.div(index, 2), z_lo))
+
+    work_peers = [works_on(lax.rem(work + by, slides)) for by in range(1, slides)]
+    members = [at_member(lax.rem(member + by, ctxs)) for by in range(1, ctxs)]
+    near = [
+        (at_slide(z_hi, x, lax.rem(core + c, 2)), at_ctx(y + yy, lax.rem(z_lo + zz, 2)))
+        for c in range(2) for yy in range(4) for zz in range(2) if (c, yy) != (0, 0)
+    ]
     barrier = pltpu.get_barrier_semaphore()
-    for peer in slide_peers + ctx_peers + [zw_pair]:
+    for peer in work_peers + near:
         pl.semaphore_signal(barrier, inc=1, device_id=peer, device_id_type=MESH)
-    pl.semaphore_wait(barrier, slides + ctxs - 1)
+    pl.semaphore_wait(barrier, len(work_peers) + len(near))
 
     def shard_of(relation, cc):
         zz = (1 - z_hi) if relation in (3, 4, 5, 7) else z_hi
@@ -156,6 +171,15 @@
     w_a[own48, 0:width] = wq[...]
     w_a[own48, width:] = wkv[...]
     gather_a.first()
+    lengths[0] = jnp.full(lengths.shape[1:], length_ref[0], jnp.int32)
+
+    def length_handle():
+        return pltpu.make_async_remote_copy(
+            src_ref=lengths.at[0], dst_ref=lengths.at[1], send_sem=l_sem.at[0],
+            recv_sem=l_sem.at[1], device_id=sibling, device_id_type=MESH,
+        )
+
+    length_handle().start()
 
     def grid(shape, dim):
         return lax.broadcasted_iota(jnp.int32, shape, dim)
@@ -177,42 +201,26 @@
     def pieces(buffer, index, depth):
         return buffer.at[pl.ds(pl.multiple_of(index * depth, 16), depth), :]
 
-    def exchange(source, target, depth, me, count, peers, send, recv):
-        def handle(by, peer):
-            return pltpu.make_async_remote_copy(
-                src_ref=pieces(source, lax.rem(me + by, count), depth),
-                dst_ref=pieces(target, me, depth), send_sem=send.at[by],
-                recv_sem=recv.at[by], device_id=peer, device_id_type=MESH,
-            )
-
-        def incoming(by, peer):
-            part = pieces(target, lax.rem(me + count - by, count), depth)
-            return pltpu.make_async_remote_copy(
-                src_ref=part, dst_ref=part, send_sem=send.at[by],
-                recv_sem=recv.at[by], device_id=peer, device_id_type=MESH,
-            )
-
-        def start():
-            for by in range(1, count):
-                handle(by, peers[by - 1]).start()
-            at = pl.ds(pl.multiple_of(me * depth, 16), depth)
-            target[at, :] = source[at, :]
-
-        def arrive():
-            for by in range(1, count):
-                incoming(by, peers[by - 1]).wait_recv()
-
-        def sent():
-            for by in range(1, count):
-                handle(by, peers[by - 1]).wait_send()
-
-        return start, arrive, sent
-
     slide_rows = block // slides
-    ctx_rows = block // ctxs
-    to_slides = exchange(outgoing, in_slide, slide_rows, slide, slides, slide_peers, s_send, s_recv)
-    to_blocks = exchange(by_ctx, in_block, ctx_rows, ctx, ctxs, ctx_peers, p_send, p_recv)
-    to_slides[0]()
+
+    def to_work(by):
+        return pltpu.make_async_remote_copy(
+            src_ref=pieces(outgoing, lax.rem(work + by, slides), slide_rows),
+            dst_ref=pieces(in_slide, work, slide_rows), send_sem=s_send.at[by],
+            recv_sem=s_recv.at[by], device_id=work_peers[by - 1], device_id_type=MESH,
+        )
+
+    def from_work(by):
+        part = pieces(in_slide, lax.rem(work + slides - by, slides), slide_rows)
+        return pltpu.make_async_remote_copy(
+            src_ref=part, dst_ref=part, send_sem=s_send.at[by],
+            recv_sem=s_recv.at[by], device_id=work_peers[by - 1], device_id_type=MESH,
+        )
+
+    for by in range(1, slides):
+        to_work(by).start()
+    own32 = pl.ds(pl.multiple_of(work * slide_rows, 16), slide_rows)
+    in_slide[own32, :] = outgoing[own32, :]
 
     w_b[own48, 0:width] = wo[...]
     w_b[own48, width:] = wu[...]
@@ -226,12 +234,12 @@
     acc[...] = jnp.zeros(acc.shape, f32)
     gather_a.second()
 
-    to_slides[1]()
+    for by in range(1, slides):
+        from_work(by).wait_recv()
     wanted = grid((block, block), 0)
     wanted = ((wanted >> 2) & 15) * slide_rows + (wanted >> 6) * share + (wanted & 3)
     turning = jnp.where(grid((block, block), 1) == wanted, 1.0, 0.0).astype(bf16)
     by_ctx[...] = dot(turning, in_slide[...]).astype(bf16)
-    to_blocks[0]()
 
     place = {key: index for index, key in enumerate(ORDER)}
 
@@ -255,29 +263,34 @@
 
     for side in range(2):
         part = slice(side * half, (side + 1) * half)
-        rows[part, :] = layer_norm(in_slide[part, 0:width], gain1[...])
-        pass_rows((0, side), 1, side, y_next)
-        pass_rows((0, side), 2, side, y_prev)
-        pass_rows((0, side), 3, side, z_pair)
+        rows[part, :] = layer_norm(by_ctx[part, 0:width], gain1[...])
+        if side == 0:
+            pass_rows((0, 0), 1, 0, y_next)
+        else:
+            pass_rows((0, 1), 2, 1, y_prev)
+            pass_rows((0, 1), 1, 1, y_next)
+            pass_rows((0, 0), 2, 0, y_prev)
+        pass_rows((0, side), 4, side, sibling)
 
     def positions(buffer):
         weight = grid((8, 128), 1)
         weight = jnp.where(weight == 0, 64.0, jnp.where(weight == 1, 1.0, 0.0)).astype(bf16)
         return dot_nt(weight, buffer[:, width:])
 
-    length = length_ref[0]
-    masked = jnp.where(positions(in_slide) >= length.astype(f32), masked_score, 0.0)
-    masks[ctx, 0] = masked[:, 0:half]
-    masks[ctx, 1] = masked[:, half:]
+    length_handle().wait()
+    valid = jnp.where(core == z_lo, lengths[0, 0:1, 0:1], lengths[1, 0:1, 0:1]).astype(f32)
+    masked = jnp.where(positions(by_ctx) >= valid, masked_score, 0.0)
+    masks[member, 0] = masked[:, 0:half]
+    masks[member, 1] = masked[:, half:]
 
     def mask_handle(by, owner):
         return pltpu.make_async_remote_copy(
             src_ref=masks.at[owner], dst_ref=masks.at[owner], send_sem=m_send.at[by],
-            recv_sem=m_recv.at[by], device_id=ctx_peers[by - 1], device_id_type=MESH,
+            recv_sem=m_recv.at[by], device_id=members[by - 1], device_id_type=MESH,
         )
 
     for by in range(1, ctxs):
-        mask_handle(by, ctx).start()
+        mask_handle(by, member).start()
 
     gather_a.third()
     gather_a.fourth()
@@ -294,13 +307,8 @@
 
     project(0)
 
-    to_blocks[1]()
-    at_row = positions(in_block)[0:1] - (ctx * block).astype(f32)
-    placing = jnp.where(grid((block, block), 0).astype(f32) == at_row, 1.0, 0.0).astype(bf16)
-    tok[...] = dot(placing, in_block[:, 0:width]).astype(bf16)
-
     scale = HEAD_DIM ** (-0.5) * 1.4426950408889634
-    queries = (dot(layer_norm(tok[...], gain1[...]), w_a[:, 0:width]) * scale).astype(bf16)
+    queries = (dot(rows[0:block, :], w_a[:, 0:width]) * scale).astype(bf16)
     queries_t = dot_nt(eye[...], queries).astype(bf16)
     for head in range(heads):
         pair, at = head // 2, head % 2
@@ -309,12 +317,11 @@
         ]
 
     for by in range(1, ctxs):
-        mask_handle(by, lax.rem(ctx + ctxs - by, ctxs)).wait_recv()
+        mask_handle(by, lax.rem(member + ctxs - by, ctxs)).wait_recv()
 
     def owner(relation):
-        step = {0: 0, 1: -1, 2: 1, 3: 0, 4: -1, 5: 1, 6: 2, 7: 2}[relation]
-        zz = (1 - z_lo) if relation in (3, 4, 5, 7) else z_lo
-        return at_ctx(y + step, zz)
+        yy = lax.rem(y + {0: 0, 1: 3, 2: 1, 3: 2}[relation % 4], 4)
+        return yy * 2 + ((1 - core) if relation >= 4 else core)
 
     def attend(first, first_side, second, second_side):
         here = jnp.concatenate([masks[first, first_side], masks[second, second_side]], axis=1)
@@ -362,49 +369,51 @@
     def turn(step, _):
         @pl.when(step == 1)
         def _():
-            for relation in (1, 2, 3):
-                rows_here(relation, 0)
-            pass_rows((1, 0), 6, 0, y_next)
-            pass_rows((3, 0), 5, 0, y_prev)
-            pass_rows((3, 0), 4, 0, y_next)
+            rows_here(4, 0)
+            rows_here(4, 1)
 
         @pl.when(step == 2)
         def _():
-            for relation in (1, 2, 3):
-                rows_here(relation, 1)
-            pass_rows((3, 1), 4, 1, y_next)
-            pass_rows((2, 1), 6, 1, y_prev)
-            pass_rows((3, 1), 5, 1, y_prev)
+            rows_here(1, 0)
+            pass_rows((1, 0), 3, 0, y_next)
+            pass_rows((1, 0), 5, 0, sibling)
+            rows_here(2, 1)
+            pass_rows((2, 1), 3, 1, y_prev)
+            pass_rows((2, 1), 6, 1, sibling)
             gather_b.second()
 
         @pl.when(step == 3)
         def _():
+            rows_here(5, 0)
+            rows_here(6, 1)
             gather_b.third()
             gather_c.first()
 
         @pl.when(step == 4)
         def _():
+            rows_here(1, 1)
+            pass_rows((1, 1), 5, 1, sibling)
+            rows_here(2, 0)
+            pass_rows((2, 0), 6, 0, sibling)
+            gather_b.fourth()
+
+        @pl.when(step == 5)
+        def _():
+            rows_here(5, 1)
             rows_here(6, 0)
-            pass_rows((6, 0), 7, 0, z_pair)
-            rows_here(5, 0)
-            gather_b.fourth()
-
-        @pl.when(step == 5)
-        def _():
-            rows_here(6, 1)
-            pass_rows((6, 1), 7, 1, z_pair)
-            rows_here(4, 0)
             gather_c.second()
 
         @pl.when(step == 6)
         def _():
+            rows_here(3, 0)
+            pass_rows((3, 0), 7, 0, sibling)
+            rows_here(3, 1)
+            pass_rows((3, 1), 7, 1, sibling)
+            gather_c.third()
+
+        @pl.when(step == 7)
+        def _():
             rows_here(7, 0)
-            rows_here(4, 1)
-            gather_c.third()
-
-        @pl.when(step == 7)
-        def _():
-            rows_here(5, 1)
             rows_here(7, 1)
             gather_c.fourth()
 
@@ -424,41 +433,95 @@
         done = acc[head]
         attended[head * 64 : head * 64 + 64, :] = (done[0:64] / done[64:65]).astype(bf16)
     turned = dot_nt(eye[0:block, 0:block], attended[...]).astype(bf16)
-    mid = (tok[...].astype(f32) + dot(turned, w_b[:, 0:width])).astype(bf16)
+    mid = (by_ctx[:, 0:width].astype(f32) + dot(turned, w_b[:, 0:width])).astype(bf16)
     for index, source in enumerate(token_sends):
         rows_handle(source, source, index, sibling).wait_send()
     rows[0:block, :] = layer_norm(mid, gain2[...])
+    down_acc[...] = mid.astype(f32)
+    finished[:, width:] = by_ctx[:, width:]
     gather_c.last()
-    down_acc[...] = mid.astype(f32)
 
     tile = up_buf.shape[2]
     tiles = hidden // tile
-
-    def up(index, slot):
-        at = pl.ds(pl.multiple_of(width + index * tile, 128), tile)
-        up_buf[slot] = dot(rows[0:block, :], w_b[:, at])
-
-    def down(index, slot):
-        active = jax.nn.gelu(up_buf[slot], approximate=True).astype(bf16)
-        down_acc[...] += dot(active, w_c[pl.ds(pl.multiple_of(index * tile, tile), tile), :])
-
-    up(0, 0)
-
-    def two_tiles(index, _):
-        up(2 * index + 1, 1)
-        down(2 * index, 0)
-        up(jnp.minimum(2 * index + 2, tiles - 1), 0)
-        down(2 * index + 1, 1)
+    part_rows = block // 4
+    ctx_rows = block // ctxs
+
+    def send_home(target_ctx):
+        return pltpu.make_async_remote_copy(
+            src_ref=pieces(finished, target_ctx, ctx_rows), dst_ref=pieces(landed, member, ctx_rows),
+            send_sem=f_send.at[target_ctx], recv_sem=f_recv.at[member],
+            device_id=(at_slide(z_hi, x, z_lo), target_ctx), device_id_type=MESH,
+        )
+
+    def from_member(index):
+        part = pieces(landed, index, ctx_rows)
+        return pltpu.make_async_remote_copy(
+            src_ref=part, dst_ref=part, send_sem=f_send.at[index], recv_sem=f_recv.at[index],
+            device_id=sibling, device_id_type=MESH,
+        )
+
+    stays = core == z_lo
+
+    def piece(index, _):
+        yy = lax.rem(y + pick([2, 1, 3, 0], index), 4)
+        here = pl.ds(pl.multiple_of(yy * part_rows, part_rows), part_rows)
+
+        def up(at, slot):
+            span = pl.ds(pl.multiple_of(width + at * tile, 128), tile)
+            up_buf[slot] = dot(rows[here, :], w_b[:, span])
+
+        def down(at, slot):
+            active = jax.nn.gelu(up_buf[slot], approximate=True).astype(bf16)
+            span = pl.ds(pl.multiple_of(at * tile, tile), tile)
+            down_acc[here, :] += dot(active, w_c[span, :])
+
+        up(0, 0)
+
+        def two_tiles(at, _):
+            up(2 * at + 1, 1)
+            down(2 * at, 0)
+            up(jnp.minimum(2 * at + 2, tiles - 1), 0)
+            down(2 * at + 1, 1)
+            return 0
+
+        lax.fori_loop(0, tiles // 2, two_tiles, 0)
+        finished[here, 0:width] = down_acc[here, :].astype(bf16)
+        for zz in range(2):
+            target = yy * 2 + zz
+            home = stays & (yy == y) & (z_lo == zz)
+
+            @pl.when(jnp.logical_not(home))
+            def _():
+                send_home(target).start()
+
+            @pl.when(home)
+            def _():
+                at = pl.ds(pl.multiple_of(member * ctx_rows, 16), ctx_rows)
+                landed[at, :] = finished[pl.ds(pl.multiple_of(target * ctx_rows, 16), ctx_rows), :]
+
         return 0
 
-    lax.fori_loop(0, tiles // 2, two_tiles, 0)
-    at = ctx * block + lax.broadcasted_iota(jnp.int32, (block, width), 0)
-    out[...] = jnp.where(at < length, down_acc[...], 0.0).astype(bf16)
-
-    to_slides[2]()
-    to_blocks[2]()
+    lax.fori_loop(0, 4, piece, 0)
+
+    for index in range(ctxs):
+        @pl.when(jnp.logical_not(stays & (member == index)))
+        def _():
+            from_member(index).wait_recv()
+
+    at_row = positions(landed)[0:1] - (ctx * block).astype(f32)
+    placing = jnp.where(grid((block, block), 0).astype(f32) == at_row, 1.0, 0.0).astype(bf16)
+    at = ctx * block + grid((block, width), 0)
+    out[...] = jnp.where(at < length_ref[0], dot(placing, landed[:, 0:width]), 0.0).astype(bf16)
+
+    for index in range(ctxs):
+        @pl.when(jnp.logical_not(stays & (ctx == index)))
+        def _():
+            send_home(index).wait_send()
+
+    for by in range(1, slides):
+        to_work(by).wait_send()
     for by in range(1, ctxs):
-        mask_handle(by, ctx).wait_send()
+        mask_handle(by, member).wait_send()
     for gather in (gather_a, gather_b, gather_c):
         gather.sent()
 
@@ -481,7 +544,8 @@
             pltpu.VMEM((block, width + 128), bf16),
             pltpu.VMEM((block, width + 128), bf16),
             pltpu.VMEM((block, width + 128), bf16),
-            pltpu.VMEM((block, width), bf16),
+            pltpu.VMEM((block, width + 128), bf16),
+            pltpu.VMEM((2, 8, 128), jnp.int32),
             pltpu.VMEM((8, 2, 8, block // 2), f32),
             pltpu.VMEM((width, width), bf16),
             pltpu.VMEM((8 * block, width), bf16),
@@ -497,11 +561,12 @@
             pltpu.VMEM((heads // 2, 1, 2 * block), f32),
             pltpu.VMEM((heads, value_rows, block), f32),
             pltpu.VMEM((width, block), bf16),
-            pltpu.VMEM((2, block, 512), f32),
+            pltpu.VMEM((2, block // 4, 512), f32),
             pltpu.VMEM((block, width), f32),
             dma((16,)), dma((16,)),
             dma((8,)), dma((8,)),
             dma((8,)), dma((8,)),
+            dma((2,)),
             dma((14,)), dma((16,)),
             dma((16,)), dma((16,)),
             dma((16,)), dma((16,)),

time: 130 us -> 126 us (0.969); the launches traced: 128 us -> 125 us
  Pallas kernels: 123 us -> 121 us
    pallas_call x1, Pallas kernels: 123 us -> 121 us  [on_device(): pl.pallas_call(layer_kernel, out_shape=jax.ShapeDtypeStruct((block, width...]
where the time goes in v3:
time: 126 us; the launch traced here: 125 us
  Pallas kernels  121 us (96%)
  local copies, waits for them, and re-layouts  3.93 us (3%)
    pallas_call x1, Pallas kernels, on_device(): pl.pallas_call(layer_kernel, out_shape=jax.ShapeDtypeStruct((block, width...  121 us

profile of v3, /device:TPU:1, one launch (start us, length us, event | category | flops | bytes accessed | tf_op | source)
XLA Modules:
  0.0 125.5 jit_solution(596377375920177095)
XLA Ops:
  0.0 0.0 copy-start
  0.7 1.3 %reshape.6.gain1 = f32[1,768]{1,0:T(1,128)} reshape(f32[768]{0:T(1024)} %param.13) | data formatting | bytes 6144 | tf_op jit(solution)/shard_map/reshape | solution.py:580
  1.9 0.0 copy-done
  1.9 0.6 reshape.7.gain2
  2.5 120.9 %layer.1 = bf16[512,768]{1,0:T(8,128)(2,1)} custom-call(bf16[512,768]{1,0:T(8,128)(2,1)} %tile_rows.1, s32[1,512]{1,0:T(1,128)} %tile_slot.1, s32[1]{0:T(128)S(6)} %copy.12.length_ref, f32[1,768]{1,0:T(1,128)} %reshape.6.gain1, bf16[48,768]{1,0:T(8,128)(2,1)} %wq.1, bf16[48,1536]{1,0:T(8,128)(2,1)} %wkv.1, bf16[48,768]{1,0:T(8,128)(2,1)} %wo.1, ...), custom_call_target="tpu_custom_call" | custom-call | tf_op jit(solution)/shard_map/layer/pallas_call | solution.py:537
  123.4 2.1 %copy.13 = bf16[512,768]{1,0:T(8,128)(2,1)} copy(bf16[512,768]{1,0:T(8,128)(2,1)} %layer.1) | data formatting | bytes 1572864
Async XLA Ops:
  0.0 1.9 %copy-start = (f32[768]{0:T(1024)S(1)}, f32[768]{0:T(1024)}, u32[]{:S(2)}) copy-start(f32[768]{0:T(1024)} %param.17) | copy-start | bytes 9220

commit v4 on v3

--- a/solution.py
+++ b/solution.py
@@ -46,7 +46,7 @@
     tile_rows, tile_slot, length_ref, gain1, wq, wkv, wo, gain2, wu, wd,
     out,
     outgoing, in_slide, by_ctx, finished, landed, lengths, masks, eye,
-    rows, w_a, w_b, w_c, w_vt, q_aug, k_buf, v_buf, bias, scores, top, acc, attended, up_buf, down_acc,
+    rows, w_a, w_b, w_c, w_vt, q_aug, k_even, k_odd, v_even, v_odd, bias_even, bias_odd, scores, top, acc, attended, up_buf, down_acc,
     s_send, s_recv, f_send, f_recv, m_send, m_recv, l_sem, t_send, t_recv, a_send, a_recv, b_send, b_recv, c_send, c_recv,
 ):
     block, width = tile_rows.shape
@@ -129,26 +129,26 @@
 
         def first(self):
             own = (0, core)
+            self.copy(own, sibling, 8)
             self.copy(own, x_next, 1)
             self.copy(own, x_prev, 2)
             self.copy(own, zw_pair, 3)
-            self.copy(own, sibling, 8)
 
         def second(self):
             for relation in (1, 2, 3):
                 self.arrive((relation, core), relation)
+            for relation in (1, 2, 3):
+                self.copy((relation, core), sibling, 8 + relation)
             self.copy((1, core, 0), x_next, 6)
             self.copy((2, core, 1), x_prev, 0)
             self.copy((3, core), x_next, 4)
             self.copy((3, core), x_prev, 5)
-            for relation in (1, 2, 3):
-                self.copy((relation, core), sibling, 8 + relation)
 
         def third(self):
             self.arrive((6, core, 0), 6)
             self.arrive((6, core, 1), 0)
+            self.copy((6, core), sibling, 14)
             self.copy((6, core), zw_pair, 7)
-            self.copy((6, core), sibling, 14)
 
         def fourth(self):
             for relation in (4, 5, 7):
@@ -229,7 +229,8 @@
     eye[...] = identity(width)
     q_aug[...] = jnp.zeros(q_aug.shape, bf16)
     q_aug[:, 128:144, :] = jnp.where(grid((pairs, 16, 2 * block), 1) == 0, 1.0, 0.0).astype(bf16)
-    v_buf[:, 64:80, :] = jnp.where(grid((heads, 16, block), 1) == 0, 1.0, 0.0).astype(bf16)
+    for v_buf in (v_even, v_odd):
+        v_buf[:, 64:80, :] = jnp.where(grid((heads, 16, block), 1) == 0, 1.0, 0.0).astype(bf16)
     top[...] = jnp.full(top.shape, masked_score, f32)
     acc[...] = jnp.zeros(acc.shape, f32)
     gather_a.second()
@@ -264,13 +265,13 @@
     for side in range(2):
         part = slice(side * half, (side + 1) * half)
         rows[part, :] = layer_norm(by_ctx[part, 0:width], gain1[...])
+        pass_rows((0, side), 4, side, sibling)
         if side == 0:
             pass_rows((0, 0), 1, 0, y_next)
         else:
             pass_rows((0, 1), 2, 1, y_prev)
             pass_rows((0, 1), 1, 1, y_next)
             pass_rows((0, 0), 2, 0, y_prev)
-        pass_rows((0, side), 4, side, sibling)
 
     def positions(buffer):
         weight = grid((8, 128), 1)
@@ -298,14 +299,19 @@
     gather_a.last()
     w_vt[...] = dot_nt(eye[...], w_a[:, 2 * width :]).astype(bf16)
 
-    def project(step):
+    k_bufs, v_bufs, biases = (k_even, k_odd), (v_even, v_odd), (bias_even, bias_odd)
+
+    def project(step, third, parity):
         here = rows[pl.ds(pl.multiple_of(step * block, block), block), :]
-        k_buf[...] = dot(here, w_a[:, width : 2 * width]).astype(bf16)
-        values_t = dot_nt(w_vt[...], here).astype(bf16)
-        for head in range(heads):
-            v_buf[head, 0:64, :] = values_t[head * 64 : head * 64 + 64, :]
-
-    project(0)
+        span = pl.ds(pl.multiple_of(third * 256, 256), 256)
+        key_span = pl.ds(pl.multiple_of(width + third * 256, 256), 256)
+        k_bufs[parity][:, span] = dot(here, w_a[:, key_span]).astype(bf16)
+        values_t = dot_nt(w_vt[span, :], here).astype(bf16)
+        for at in range(4):
+            v_bufs[parity][4 * third + at, 0:64, :] = values_t[at * 64 : at * 64 + 64, :]
+
+    for third in range(3):
+        project(0, third, 0)
 
     scale = HEAD_DIM ** (-0.5) * 1.4426950408889634
     queries = (dot(rows[0:block, :], w_a[:, 0:width]) * scale).astype(bf16)
@@ -323,36 +329,25 @@
         yy = lax.rem(y + {0: 0, 1: 3, 2: 1, 3: 2}[relation % 4], 4)
         return yy * 2 + ((1 - core) if relation >= 4 else core)
 
-    def attend(first, first_side, second, second_side):
+    def mask_column(first, first_side, second, second_side, parity):
         here = jnp.concatenate([masks[first, first_side], masks[second, second_side]], axis=1)
         here = jnp.concatenate([here, jnp.zeros((120, block), f32)], axis=0).astype(bf16)
-        bias[...] = dot_nt(eye[0:block, 0:block], here).astype(bf16)
-
-        def score(pair, slot):
-            keys = k_buf[:, pl.ds(pl.multiple_of(pair * 128, 128), 128)]
-            scores[slot] = dot(jnp.concatenate([keys, bias[...]], axis=1), q_aug[pair])
-
-        def soften(pair, slot):
-            before = top[pair]
-            now = jnp.maximum(before, jnp.max(scores[slot], axis=0, keepdims=True))
-            factor = jnp.exp2(before - now)
-            top[pair] = now
-            for side in range(2):
-                span = slice(side * block, (side + 1) * block)
-                weights = jnp.exp2(scores[slot, :, span] - now[:, span]).astype(bf16)
-                head = 2 * pair + side
-                acc[head] = acc[head] * factor[:, span] + dot(v_buf[head], weights)
-
-        score(0, 0)
-
-        def two(index, _):
-            score(2 * index + 1, 1)
-            soften(2 * index, 0)
-            score(jnp.minimum(2 * index + 2, pairs - 1), 0)
-            soften(2 * index + 1, 1)
-            return 0
-
-        lax.fori_loop(0, pairs // 2, two, 0)
+        biases[parity][...] = dot_nt(eye[0:block, 0:block], here).astype(bf16)
+
+    def score(pair, slot, parity):
+        keys = k_bufs[parity][:, pl.ds(pl.multiple_of(pair * 128, 128), 128)]
+        scores[slot] = dot(jnp.concatenate([keys, biases[parity][...]], axis=1), q_aug[pair])
+
+    def soften(pair, slot, parity):
+        before = top[pair]
+        now = jnp.maximum(before, jnp.max(scores[slot], axis=0, keepdims=True))
+        factor = jnp.exp2(before - now)
+        top[pair] = now
+        for side in range(2):
+            span = slice(side * block, (side + 1) * block)
+            weights = jnp.exp2(scores[slot, :, span] - now[:, span]).astype(bf16)
+            head = 2 * pair + side
+            acc[head] = acc[head] * factor[:, span] + dot(v_bufs[parity][head], weights)
 
     steps = len(ORDER) // 2
     firsts = [owner(ORDER[2 * step][0]) for step in range(steps)]
@@ -366,67 +361,83 @@
             chosen = jnp.where(step == index, options[index], chosen)
         return chosen
 
-    def turn(step, _):
-        @pl.when(step == 1)
-        def _():
-            rows_here(4, 0)
-            rows_here(4, 1)
-
-        @pl.when(step == 2)
-        def _():
-            rows_here(1, 0)
-            pass_rows((1, 0), 3, 0, y_next)
-            pass_rows((1, 0), 5, 0, sibling)
-            rows_here(2, 1)
-            pass_rows((2, 1), 3, 1, y_prev)
-            pass_rows((2, 1), 6, 1, sibling)
-            gather_b.second()
-
-        @pl.when(step == 3)
-        def _():
-            rows_here(5, 0)
-            rows_here(6, 1)
-            gather_b.third()
-            gather_c.first()
-
-        @pl.when(step == 4)
-        def _():
-            rows_here(1, 1)
-            pass_rows((1, 1), 5, 1, sibling)
-            rows_here(2, 0)
-            pass_rows((2, 0), 6, 0, sibling)
-            gather_b.fourth()
-
-        @pl.when(step == 5)
-        def _():
-            rows_here(5, 1)
-            rows_here(6, 0)
-            gather_c.second()
-
-        @pl.when(step == 6)
-        def _():
-            rows_here(3, 0)
-            pass_rows((3, 0), 7, 0, sibling)
-            rows_here(3, 1)
-            pass_rows((3, 1), 7, 1, sibling)
-            gather_c.third()
-
-        @pl.when(step == 7)
-        def _():
-            rows_here(7, 0)
-            rows_here(7, 1)
-            gather_c.fourth()
-
-        @pl.when(step > 0)
-        def _():
-            project(step)
-
-        attend(
-            pick(firsts, step), pick(first_sides, step), pick(seconds, step), pick(second_sides, step)
-        )
+    def mask_of(step, parity):
+        mask_column(
+            pick(firsts, step), pick(first_sides, step), pick(seconds, step), pick(second_sides, step),
+            parity,
+        )
+
+    def step_0():
+        rows_here(4, 0)
+        rows_here(4, 1)
+
+    def step_1():
+        rows_here(1, 0)
+        pass_rows((1, 0), 5, 0, sibling)
+        pass_rows((1, 0), 3, 0, y_next)
+        rows_here(2, 1)
+        pass_rows((2, 1), 6, 1, sibling)
+        pass_rows((2, 1), 3, 1, y_prev)
+
+    def step_2():
+        rows_here(5, 0)
+        rows_here(6, 1)
+        gather_b.second()
+
+    def step_3():
+        rows_here(1, 1)
+        pass_rows((1, 1), 5, 1, sibling)
+        rows_here(2, 0)
+        pass_rows((2, 0), 6, 0, sibling)
+        gather_b.third()
+        gather_c.first()
+
+    def step_4():
+        rows_here(5, 1)
+        rows_here(6, 0)
+        gather_b.fourth()
+
+    def step_5():
+        rows_here(3, 0)
+        pass_rows((3, 0), 7, 0, sibling)
+        rows_here(3, 1)
+        pass_rows((3, 1), 7, 1, sibling)
+        gather_c.second()
+
+    def step_6():
+        rows_here(7, 0)
+        rows_here(7, 1)
+        gather_c.third()
+
+    def step_7():
+        gather_c.fourth()
+
+    events = [step_0, step_1, step_2, step_3, step_4, step_5, step_6, step_7]
+
+    def turn(step, parity):
+        for index in range(parity, steps, 2):
+            pl.when(step == index)(events[index])
+        later = jnp.minimum(step + 1, steps - 1)
+        mask_of(later, 1 - parity)
+
+        for third in range(3):
+            project(later, third, 1 - parity)
+            score(2 * third + 1, 1, parity)
+            soften(2 * third, 0, parity)
+            if third < 2:
+                score(2 * third + 2, 0, parity)
+            else:
+                score(0, 0, 1 - parity)
+            soften(2 * third + 1, 1, parity)
+
+    def two_steps(index, _):
+        turn(2 * index, 0)
+        turn(2 * index + 1, 1)
         return 0
 
-    lax.fori_loop(0, steps, turn, 0)
+    mask_of(0, 0)
+    score(0, 0, 0)
+    lax.fori_loop(0, steps // 2, two_steps, 0)
 
     gather_b.last()
     for head in range(heads):
@@ -555,7 +566,10 @@
             pltpu.VMEM((width, width), bf16),
             pltpu.VMEM((heads // 2, 256, 2 * block), bf16),
             pltpu.VMEM((block, width), bf16),
+            pltpu.VMEM((block, width), bf16),
             pltpu.VMEM((heads, value_rows, block), bf16),
+            pltpu.VMEM((heads, value_rows, block), bf16),
+            pltpu.VMEM((block, 128), bf16),
             pltpu.VMEM((block, 128), bf16),
             pltpu.VMEM((2, block, 2 * block), f32),
             pltpu.VMEM((heads // 2, 1, 2 * block), f32),
@@ -577,8 +591,8 @@
         ),
         name="layer",
     )(
-        tile_rows, tile_slot, lengths, ln_gain_attn.reshape(1, width), w_query, w_kv, w_out,
-        ln_gain_mlp.reshape(1, width), w_up, w_down,
+        tile_rows, tile_slot, lengths, ln_gain_attn, w_query, w_kv, w_out,
+        ln_gain_mlp, w_up, w_down,
     )
 
 

time: 126 us -> 120 us (0.952)
  Pallas kernels: 121 us -> 117 us
  local copies, waits for them, and re-layouts: 3.93 us -> 2.06 us
    pallas_call x1, Pallas kernels: 121 us -> 117 us  [on_device(): pl.pallas_call(layer_kernel, out_shape=jax.ShapeDtypeStruct((block, width...]
    reshape x2 -> x0, local copies, waits for them, and re-layouts: 1.86 us -> none  [the longest x1 1.27 us: on_device(): ln_gain_attn.reshape(1, width)]
where the time goes in v4:
time: 120 us
  Pallas kernels  117 us (98%)
  local copies, waits for them, and re-layouts  2.06 us (2%)
    pallas_call x1, Pallas kernels, on_device(): pl.pallas_call(layer_kernel, out_shape=jax.ShapeDtypeStruct((block, width...  117 us

profile of v4, /device:TPU:1, one launch (start us, length us, event | category | flops | bytes accessed | tf_op | source)
XLA Modules:
  0.0 120.0 jit_solution(15775179641518331286)
XLA Ops:
  0.7 117.2 %layer.1 = bf16[512,768]{1,0:T(8,128)(2,1)} custom-call(bf16[512,768]{1,0:T(8,128)(2,1)} %tile_rows.1, s32[1,512]{1,0:T(1,128)} %tile_slot.1, s32[1]{0:T(128)S(6)} %copy.12.length_ref, f32[768]{0:T(1024)} %gain1.1, bf16[48,768]{1,0:T(8,128)(2,1)} %wq.1, bf16[48,1536]{1,0:T(8,128)(2,1)} %wkv.1, bf16[48,768]{1,0:T(8,128)(2,1)} %wo.1, f32[768]{0:T(1024)} %gain2.1, ...), custom_call_target="tpu_custom_call" | custom-call | tf_op jit(solution)/shard_map/layer/pallas_call | solution.py:548
  117.9 2.1 %copy.13 = bf16[512,768]{1,0:T(8,128)(2,1)} copy(bf16[512,768]{1,0:T(8,128)(2,1)} %layer.1) | data formatting | bytes 1572864

commit v5 on v4

--- a/solution.py
+++ b/solution.py
@@ -101,17 +101,23 @@
         step = {0: 0, 1: -1, 2: 1, 3: 0, 4: -1, 5: 1, 6: 2, 7: 2}[relation]
         return at_slide(zz, x + step, cc)
 
+    x_far = (at_slide(z_hi, x + 2, core), ctx)
+
     class Gather:
-        def __init__(self, whole, depth, send, recv):
+        def __init__(self, whole, depth, send, recv, direct, split):
             self.whole, self.depth, self.send, self.recv = whole, depth, send, recv
+            self.direct, self.split = direct, split
             self.started = []
 
-        def part(self, relation, cc, side=None):
+        def part(self, relation, cc, columns):
             at = pl.ds(pl.multiple_of(shard_of(relation, cc) * self.depth, 16), self.depth)
-            if side is None:
+            cut = self.whole.shape[1] // 2
+            if columns == "all" or (columns == "mine" and not self.split):
                 return self.whole.at[at, :]
-            cut = self.whole.shape[1] // 2
-            return self.whole.at[at, pl.ds(side * cut, cut)]
+            if columns in (0, 1):
+                return self.whole.at[at, pl.ds(columns * cut, cut)]
+            side = lax.rem(y, 2) if columns == "mine" else 1 - lax.rem(y, 2)
+            return self.whole.at[at, pl.ds(pl.multiple_of(side * cut, 128), cut)]
 
         def handle(self, key, send_slot, slot, peer):
             part = self.part(*key)
@@ -127,45 +133,66 @@
         def arrive(self, key, slot):
             self.handle(key, 0, slot, sibling).wait_recv()
 
+        def share(self, relation):
+            key = (relation, core, "mine")
+            self.copy(key, sibling, 8 + relation)
+            if self.split:
+                self.copy(key, y_next if relation % 2 else y_prev, 16 + relation)
+
         def first(self):
-            own = (0, core)
-            self.copy(own, sibling, 8)
+            self.copy((0, core, "all"), sibling, 8)
+            own = (0, core, "mine")
             self.copy(own, x_next, 1)
             self.copy(own, x_prev, 2)
             self.copy(own, zw_pair, 3)
+            if self.direct:
+                self.copy(own, x_far, 6)
 
         def second(self):
             for relation in (1, 2, 3):
-                self.arrive((relation, core), relation)
-            for relation in (1, 2, 3):
-                self.copy((relation, core), sibling, 8 + relation)
-            self.copy((1, core, 0), x_next, 6)
-            self.copy((2, core, 1), x_prev, 0)
-            self.copy((3, core), x_next, 4)
-            self.copy((3, core), x_prev, 5)
+                self.arrive((relation, core, "mine"), relation)
+                self.share(relation)
+            if not self.direct:
+                self.copy((1, core, 0), x_next, 6)
+                self.copy((2, core, 1), x_prev, 0)
+            self.copy((3, core, "mine"), x_next, 4)
+            self.copy((3, core, "mine"), x_prev, 5)
+            if self.direct:
+                self.third()
 
         def third(self):
-            self.arrive((6, core, 0), 6)
-            self.arrive((6, core, 1), 0)
-            self.copy((6, core), sibling, 14)
-            self.copy((6, core), zw_pair, 7)
+            if self.direct:
+                self.arrive((6, core, "mine"), 6)
+            else:
+                self.arrive((6, core, 0), 6)
+                self.arrive((6, core, 1), 0)
+            self.share(6)
+            self.copy((6, core, "mine"), zw_pair, 7)
 
         def fourth(self):
             for relation in (4, 5, 7):
-                self.arrive((relation, core), relation)
-                self.copy((relation, core), sibling, 8 + relation)
+                self.arrive((relation, core, "mine"), relation)
+                self.share(relation)
+
+        def fifth(self):
+            for relation in range(1, 8):
+                self.arrive((relation, core, "other"), 16 + relation)
+                self.copy((relation, core, "other"), sibling, 24 + relation)
 
         def last(self):
-            for relation in range(8):
-                self.arrive((relation, 1 - core), 8 + relation)
+            self.arrive((0, 1 - core, "all"), 8)
+            for relation in range(1, 8):
+                self.arrive((relation, 1 - core, "mine"), 8 + relation)
+                if self.split:
+                    self.arrive((relation, 1 - core, "other"), 24 + relation)
 
         def sent(self):
             for index, key in enumerate(self.started):
                 self.handle(key, index, 0, sibling).wait_send()
 
-    gather_a = Gather(w_a, wq.shape[0], a_send, a_recv)
-    gather_b = Gather(w_b, wu.shape[0], b_send, b_recv)
-    gather_c = Gather(w_c, wd.shape[0], c_send, c_recv)
+    gather_a = Gather(w_a, wq.shape[0], a_send, a_recv, True, True)
+    gather_b = Gather(w_b, wu.shape[0], b_send, b_recv, False, False)
+    gather_c = Gather(w_c, wd.shape[0], c_send, c_recv, True, False)
 
     own48 = pl.ds(pl.multiple_of(slide * wq.shape[0], 16), wq.shape[0])
     w_a[own48, 0:width] = wq[...]
@@ -270,8 +297,6 @@
             pass_rows((0, 0), 1, 0, y_next)
         else:
             pass_rows((0, 1), 2, 1, y_prev)
-            pass_rows((0, 1), 1, 1, y_next)
-            pass_rows((0, 0), 2, 0, y_prev)
 
     def positions(buffer):
         weight = grid((8, 128), 1)
@@ -293,9 +318,9 @@
     for by in range(1, ctxs):
         mask_handle(by, member).start()
 
-    gather_a.third()
     gather_a.fourth()
     gather_b.first()
+    gather_a.fifth()
     gather_a.last()
     w_vt[...] = dot_nt(eye[...], w_a[:, 2 * width :]).astype(bf16)
 
@@ -370,6 +395,9 @@
     def step_0():
         rows_here(4, 0)
         rows_here(4, 1)
+        pass_rows((0, 1), 1, 1, y_next)
+        pass_rows((0, 0), 2, 0, y_prev)
+        gather_c.first()
 
     def step_1():
         rows_here(1, 0)
@@ -389,28 +417,25 @@
         pass_rows((1, 1), 5, 1, sibling)
         rows_here(2, 0)
         pass_rows((2, 0), 6, 0, sibling)
-        gather_b.third()
-        gather_c.first()
 
     def step_4():
         rows_here(5, 1)
         rows_here(6, 0)
-        gather_b.fourth()
+        gather_c.second()
 
     def step_5():
         rows_here(3, 0)
         pass_rows((3, 0), 7, 0, sibling)
         rows_here(3, 1)
         pass_rows((3, 1), 7, 1, sibling)
-        gather_c.second()
 
     def step_6():
         rows_here(7, 0)
         rows_here(7, 1)
-        gather_c.third()
+        gather_b.third()
 
     def step_7():
-        gather_c.fourth()
+        pass
 
     events = [step_0, step_1, step_2, step_3, step_4, step_5, step_6, step_7]
 
@@ -439,10 +464,12 @@
     score(0, 0, 0)
     lax.fori_loop(0, steps // 2, two_steps, 0)
 
-    gather_b.last()
+    gather_b.fourth()
+    gather_c.fourth()
     for head in range(heads):
         done = acc[head]
         attended[head * 64 : head * 64 + 64, :] = (done[0:64] / done[64:65]).astype(bf16)
+    gather_b.last()
     turned = dot_nt(eye[0:block, 0:block], attended[...]).astype(bf16)
     mid = (by_ctx[:, 0:width].astype(f32) + dot(turned, w_b[:, 0:width])).astype(bf16)
     for index, source in enumerate(token_sends):
@@ -582,7 +609,7 @@
             dma((8,)), dma((8,)),
             dma((2,)),
             dma((14,)), dma((16,)),
-            dma((16,)), dma((16,)),
+            dma((32,)), dma((32,)),
             dma((16,)), dma((16,)),
             dma((16,)), dma((16,)),
         ],

time: 120 us -> 113 us (0.942)
  Pallas kernels: 117 us -> 109 us
    pallas_call x1, Pallas kernels: 117 us -> 109 us  [on_device(): pl.pallas_call(layer_kernel, out_shape=jax.ShapeDtypeStruct((block, width...]
where the time goes in v5:
time: 113 us; the launch traced here: 112 us
  Pallas kernels  109 us (96%)
  local copies, waits for them, and re-layouts  2.06 us (2%)
    pallas_call x1, Pallas kernels, on_device(): pl.pallas_call(layer_kernel, out_shape=jax.ShapeDtypeStruct((block, width...  109 us

profile of v5, /device:TPU:1, one launch (start us, length us, event | category | flops | bytes accessed | tf_op | source)
XLA Modules:
  0.0 112.0 jit_solution(11769731647067746660)
XLA Ops:
  0.7 109.3 %layer.1 = bf16[512,768]{1,0:T(8,128)(2,1)} custom-call(bf16[512,768]{1,0:T(8,128)(2,1)} %tile_rows.1, s32[1,512]{1,0:T(1,128)} %tile_slot.1, s32[1]{0:T(128)S(6)} %copy.12.length_ref, f32[768]{0:T(1024)} %gain1.1, bf16[48,768]{1,0:T(8,128)(2,1)} %wq.1, bf16[48,1536]{1,0:T(8,128)(2,1)} %wkv.1, bf16[48,768]{1,0:T(8,128)(2,1)} %wo.1, f32[768]{0:T(1024)} %gain2.1, ...), custom_call_target="tpu_custom_call" | custom-call | tf_op jit(solution)/shard_map/layer/pallas_call | solution.py:575
  110.0 2.1 %copy.13 = bf16[512,768]{1,0:T(8,128)(2,1)} copy(bf16[512,768]{1,0:T(8,128)(2,1)} %layer.1) | data formatting | bytes 1572864

commit v6 on v5

--- a/solution.py
+++ b/solution.py
@@ -94,7 +94,6 @@
     barrier = pltpu.get_barrier_semaphore()
     for peer in work_peers + near:
         pl.semaphore_signal(barrier, inc=1, device_id=peer, device_id_type=MESH)
-    pl.semaphore_wait(barrier, len(work_peers) + len(near))
 
     def shard_of(relation, cc):
         zz = (1 - z_hi) if relation in (3, 4, 5, 7) else z_hi
@@ -197,17 +196,6 @@
     own48 = pl.ds(pl.multiple_of(slide * wq.shape[0], 16), wq.shape[0])
     w_a[own48, 0:width] = wq[...]
     w_a[own48, width:] = wkv[...]
-    gather_a.first()
-    lengths[0] = jnp.full(lengths.shape[1:], length_ref[0], jnp.int32)
-
-    def length_handle():
-        return pltpu.make_async_remote_copy(
-            src_ref=lengths.at[0], dst_ref=lengths.at[1], send_sem=l_sem.at[0],
-            recv_sem=l_sem.at[1], device_id=sibling, device_id_type=MESH,
-        )
-
-    length_handle().start()
-
     def grid(shape, dim):
         return lax.broadcasted_iota(jnp.int32, shape, dim)
 
@@ -225,6 +213,18 @@
     outgoing[:, 0:width] = dot(sorting, tile_rows[...]).astype(bf16)
     outgoing[:, width:] = dot_nt(sorting, digits.astype(f32).astype(bf16)).astype(bf16)
 
+    pl.semaphore_wait(barrier, len(work_peers) + len(near))
+    gather_a.first()
+    lengths[0] = jnp.full(lengths.shape[1:], length_ref[0], jnp.int32)
+
+    def length_handle():
+        return pltpu.make_async_remote_copy(
+            src_ref=lengths.at[0], dst_ref=lengths.at[1], send_sem=l_sem.at[0],
+            recv_sem=l_sem.at[1], device_id=sibling, device_id_type=MESH,
+        )
+
+    length_handle().start()
+
     def pieces(buffer, index, depth):
         return buffer.at[pl.ds(pl.multiple_of(index * depth, 16), depth), :]
 
@@ -260,7 +260,9 @@
         v_buf[:, 64:80, :] = jnp.where(grid((heads, 16, block), 1) == 0, 1.0, 0.0).astype(bf16)
     top[...] = jnp.full(top.shape, masked_score, f32)
     acc[...] = jnp.zeros(acc.shape, f32)
+
     gather_a.second()
+    gather_a.fourth()
 
     for by in range(1, slides):
         from_work(by).wait_recv()
@@ -318,9 +320,8 @@
     for by in range(1, ctxs):
         mask_handle(by, member).start()
 
-    gather_a.fourth()
+    gather_a.fifth()
     gather_b.first()
-    gather_a.fifth()
     gather_a.last()
     w_vt[...] = dot_nt(eye[...], w_a[:, 2 * width :]).astype(bf16)
 

time: 113 us -> 109 us (0.965)
  Pallas kernels: 109 us -> 106 us
    pallas_call x1, Pallas kernels: 109 us -> 106 us  [on_device(): pl.pallas_call(layer_kernel, out_shape=jax.ShapeDtypeStruct((block, width...]
where the time goes in v6:
time: 109 us
  Pallas kernels  106 us (97%)
  local copies, waits for them, and re-layouts  2.06 us (2%)
    pallas_call x1, Pallas kernels, on_device(): pl.pallas_call(layer_kernel, out_shape=jax.ShapeDtypeStruct((block, width...  106 us

profile of v6, /device:TPU:1, one launch (start us, length us, event | category | flops | bytes accessed | tf_op | source)
XLA Modules:
  0.0 109.1 jit_solution(3971809892888535336)
XLA Ops:
  0.7 106.4 %layer.1 = bf16[512,768]{1,0:T(8,128)(2,1)} custom-call(bf16[512,768]{1,0:T(8,128)(2,1)} %tile_rows.1, s32[1,512]{1,0:T(1,128)} %tile_slot.1, s32[1]{0:T(128)S(6)} %copy.12.length_ref, f32[768]{0:T(1024)} %gain1.1, bf16[48,768]{1,0:T(8,128)(2,1)} %wq.1, bf16[48,1536]{1,0:T(8,128)(2,1)} %wkv.1, bf16[48,768]{1,0:T(8,128)(2,1)} %wo.1, f32[768]{0:T(1024)} %gain2.1, ...), custom_call_target="tpu_custom_call" | custom-call | tf_op jit(solution)/shard_map/layer/pallas_call | solution.py:576
  107.1 2.1 %copy.13 = bf16[512,768]{1,0:T(8,128)(2,1)} copy(bf16[512,768]{1,0:T(8,128)(2,1)} %layer.1) | data formatting | bytes 1572864

commit v7 on v6

--- a/solution.py
+++ b/solution.py
@@ -45,9 +45,9 @@
 def layer_kernel(
     tile_rows, tile_slot, length_ref, gain1, wq, wkv, wo, gain2, wu, wd,
     out,
-    outgoing, in_slide, by_ctx, finished, landed, lengths, masks, eye,
+    outgoing, in_slide, by_ctx, finished, landed, landed_at, lengths, masks, eye,
     rows, w_a, w_b, w_c, w_vt, q_aug, k_even, k_odd, v_even, v_odd, bias_even, bias_odd, scores, top, acc, attended, up_buf, down_acc,
-    s_send, s_recv, f_send, f_recv, m_send, m_recv, l_sem, t_send, t_recv, a_send, a_recv, b_send, b_recv, c_send, c_recv,
+    s_send, s_recv, f_send, f_recv, i_send, i_recv, m_send, m_recv, l_sem, t_send, t_recv, a_send, a_recv, b_send, b_recv, c_send, c_recv,
 ):
     block, width = tile_rows.shape
     half = block // 2
@@ -303,11 +303,11 @@
     def positions(buffer):
         weight = grid((8, 128), 1)
         weight = jnp.where(weight == 0, 64.0, jnp.where(weight == 1, 1.0, 0.0)).astype(bf16)
-        return dot_nt(weight, buffer[:, width:])
+        return dot_nt(weight, buffer)
 
     length_handle().wait()
     valid = jnp.where(core == z_lo, lengths[0, 0:1, 0:1], lengths[1, 0:1, 0:1]).astype(f32)
-    masked = jnp.where(positions(by_ctx) >= valid, masked_score, 0.0)
+    masked = jnp.where(positions(by_ctx[:, width:]) >= valid, masked_score, 0.0)
     masks[member, 0] = masked[:, 0:half]
     masks[member, 1] = masked[:, half:]
 
@@ -319,6 +319,27 @@
 
     for by in range(1, ctxs):
         mask_handle(by, member).start()
+
+    ctx_rows = block // ctxs
+    stays = core == z_lo
+
+    def send_places(target_ctx):
+        at = pl.ds(pl.multiple_of(target_ctx * ctx_rows, 16), ctx_rows)
+        return pltpu.make_async_remote_copy(
+            src_ref=by_ctx.at[at, pl.ds(width, 128)], dst_ref=pieces(landed_at, member, ctx_rows),
+            send_sem=i_send.at[target_ctx], recv_sem=i_recv.at[member],
+            device_id=(at_slide(z_hi, x, z_lo), target_ctx), device_id_type=MESH,
+        )
+
+    for index in range(ctxs):
+        @pl.when(jnp.logical_not(stays & (ctx == index)))
+        def _():
+            send_places(index).start()
+
+    @pl.when(stays)
+    def _():
+        at = pl.ds(pl.multiple_of(member * ctx_rows, 16), ctx_rows)
+        landed_at[at, :] = by_ctx[pl.ds(pl.multiple_of(ctx * ctx_rows, 16), ctx_rows), width:]
 
     gather_a.fifth()
     gather_b.first()
@@ -403,12 +424,12 @@
     def step_1():
         rows_here(1, 0)
         pass_rows((1, 0), 5, 0, sibling)
-        pass_rows((1, 0), 3, 0, y_next)
         rows_here(2, 1)
         pass_rows((2, 1), 6, 1, sibling)
+
+    def step_2():
+        pass_rows((1, 0), 3, 0, y_next)
         pass_rows((2, 1), 3, 1, y_prev)
-
-    def step_2():
         rows_here(5, 0)
         rows_here(6, 1)
         gather_b.second()
@@ -465,11 +486,11 @@
     score(0, 0, 0)
     lax.fori_loop(0, steps // 2, two_steps, 0)
 
-    gather_b.fourth()
-    gather_c.fourth()
     for head in range(heads):
         done = acc[head]
         attended[head * 64 : head * 64 + 64, :] = (done[0:64] / done[64:65]).astype(bf16)
+    gather_b.fourth()
+    gather_c.fourth()
     gather_b.last()
     turned = dot_nt(eye[0:block, 0:block], attended[...]).astype(bf16)
     mid = (by_ctx[:, 0:width].astype(f32) + dot(turned, w_b[:, 0:width])).astype(bf16)
@@ -477,13 +498,11 @@
         rows_handle(source, source, index, sibling).wait_send()
     rows[0:block, :] = layer_norm(mid, gain2[...])
     down_acc[...] = mid.astype(f32)
-    finished[:, width:] = by_ctx[:, width:]
     gather_c.last()
 
     tile = up_buf.shape[2]
     tiles = hidden // tile
     part_rows = block // 4
-    ctx_rows = block // ctxs
 
     def send_home(target_ctx):
         return pltpu.make_async_remote_copy(
@@ -492,14 +511,12 @@
             device_id=(at_slide(z_hi, x, z_lo), target_ctx), device_id_type=MESH,
         )
 
-    def from_member(index):
-        part = pieces(landed, index, ctx_rows)
-        return pltpu.make_async_remote_copy(
-            src_ref=part, dst_ref=part, send_sem=f_send.at[index], recv_sem=f_recv.at[index],
+    def from_member(index, buffer, send, recv):
+        part = pieces(buffer, index, ctx_rows)
+        return pltpu.make_async_remote_copy(
+            src_ref=part, dst_ref=part, send_sem=send.at[index], recv_sem=recv.at[index],
             device_id=sibling, device_id_type=MESH,
         )
-
-    stays = core == z_lo
 
     def piece(index, _):
         yy = lax.rem(y + pick([2, 1, 3, 0], index), 4)
@@ -524,7 +541,7 @@
             return 0
 
         lax.fori_loop(0, tiles // 2, two_tiles, 0)
-        finished[here, 0:width] = down_acc[here, :].astype(bf16)
+        finished[here, :] = down_acc[here, :].astype(bf16)
         for zz in range(2):
             target = yy * 2 + zz
             home = stays & (yy == y) & (z_lo == zz)
@@ -545,16 +562,18 @@
     for index in range(ctxs):
         @pl.when(jnp.logical_not(stays & (member == index)))
         def _():
-            from_member(index).wait_recv()
-
-    at_row = positions(landed)[0:1] - (ctx * block).astype(f32)
+            from_member(index, landed_at, i_send, i_recv).wait_recv()
+            from_member(index, landed, f_send, f_recv).wait_recv()
+
+    at_row = positions(landed_at[...])[0:1] - (ctx * block).astype(f32)
     placing = jnp.where(grid((block, block), 0).astype(f32) == at_row, 1.0, 0.0).astype(bf16)
     at = ctx * block + grid((block, width), 0)
-    out[...] = jnp.where(at < length_ref[0], dot(placing, landed[:, 0:width]), 0.0).astype(bf16)
+    out[...] = jnp.where(at < length_ref[0], dot(placing, landed[...]), 0.0).astype(bf16)
 
     for index in range(ctxs):
         @pl.when(jnp.logical_not(stays & (ctx == index)))
         def _():
+            send_places(index).wait_send()
             send_home(index).wait_send()
 
     for by in range(1, slides):
@@ -582,8 +601,9 @@
             pltpu.VMEM((block, width + 128), bf16),
             pltpu.VMEM((block, width + 128), bf16),
             pltpu.VMEM((block, width + 128), bf16),
-            pltpu.VMEM((block, width + 128), bf16),
-            pltpu.VMEM((block, width + 128), bf16),
+            pltpu.VMEM((block, width), bf16),
+            pltpu.VMEM((block, width), bf16),
+            pltpu.VMEM((block, 128), bf16),
             pltpu.VMEM((2, 8, 128), jnp.int32),
             pltpu.VMEM((8, 2, 8, block // 2), f32),
             pltpu.VMEM((width, width), bf16),
@@ -608,6 +628,7 @@
             dma((16,)), dma((16,)),
             dma((8,)), dma((8,)),
             dma((8,)), dma((8,)),
+            dma((8,)), dma((8,)),
             dma((2,)),
             dma((14,)), dma((16,)),
             dma((32,)), dma((32,)),

time: 109 us -> 109 us (level)
  no operation moved by 1% of the time
where the time goes in v7:
time: 109 us; the launch traced here: 108 us
  Pallas kernels  106 us (97%)
  local copies, waits for them, and re-layouts  2.06 us (2%)
    pallas_call x1, Pallas kernels, on_device(): pl.pallas_call(layer_kernel, out_shape=jax.ShapeDtypeStruct((block, width...  106 us

profile of v7, /device:TPU:1, one launch (start us, length us, event | category | flops | bytes accessed | tf_op | source)
XLA Modules:
  0.0 108.4 jit_solution(1503351852651509989)
XLA Ops:
  0.7 105.7 %layer.1 = bf16[512,768]{1,0:T(8,128)(2,1)} custom-call(bf16[512,768]{1,0:T(8,128)(2,1)} %tile_rows.1, s32[1,512]{1,0:T(1,128)} %tile_slot.1, s32[1]{0:T(128)S(6)} %copy.12.length_ref, f32[768]{0:T(1024)} %gain1.1, bf16[48,768]{1,0:T(8,128)(2,1)} %wq.1, bf16[48,1536]{1,0:T(8,128)(2,1)} %wkv.1, bf16[48,768]{1,0:T(8,128)(2,1)} %wo.1, f32[768]{0:T(1024)} %gain2.1, ...), custom_call_target="tpu_custom_call" | custom-call | tf_op jit(solution)/shard_map/layer/pallas_call | solution.py:595
  106.4 2.1 %copy.13 = bf16[512,768]{1,0:T(8,128)(2,1)} copy(bf16[512,768]{1,0:T(8,128)(2,1)} %layer.1) | data formatting | bytes 1572864
